TPU v7x, 32 devices: a whole 2x2x4 slice. The times are simulated.
32 devices in a mesh: dp: 16 (over z, y, x), head: 2 (over core).
Axes of the slice: x: 2, y: 2, z: 4, core: 2. Of those that a mesh axis runs over, the one named last changes fastest.
Arguments:
- inputs: bfloat16 [64, 1024, 768], P('dp', None, 'head'), may hold values from -6 to 6
- lengths: int32 [64], P('dp'), may hold values from 64 to 1024, as said below
- gain_mix: bfloat16 [768], P('dp'), may hold values from 0.5 to 1.5
- w_value: bfloat16 [768, 768], P('dp', 'head'), may hold values from -0.21875 to 0.21875
- mix_table: bfloat16 [12, 1024, 1024], P('head', 'dp'), may hold values from -6 to 6
- w_out: bfloat16 [768, 768], P('head', 'dp'), may hold values from -1.5 to 1.5
- gain_feed: bfloat16 [768], P('dp'), may hold values from 0.5 to 1.5
- w_up: bfloat16 [768, 3072], P('dp', 'head'), may hold values from -0.21875 to 0.21875
- w_down: bfloat16 [3072, 768], P('head', 'dp'), may hold values from -0.109375 to 0.109375
- out_grad: bfloat16 [64, 1024, 768], P('dp', None, 'head'), may hold values from -6 to 6
Outputs:
- output: bfloat16 [64, 1024, 768], P('dp', None, 'head')
- input_grad: bfloat16 [64, 1024, 768], P('dp', None, 'head')
- gain_mix_grad: float32 [768], P('dp')
- value_grad: float32 [768, 768], P('dp', 'head')
- table_grad: float32 [12, 1024, 1024], P('head', 'dp')
- projection_grad: float32 [768, 768], P('head', 'dp')
- gain_feed_grad: float32 [768], P('dp')
- up_grad: float32 [768, 3072], P('dp', 'head')
- down_grad: float32 [3072, 768], P('head', 'dp')
Inputs may be any that keep to these rules, and one draw needn't show every extreme that they name: `lengths`: each item's valid length; positions at or past it are padding. In every draw some item has exactly 1024 and some other exactly 64.
All inputs are finite; a program needn't handle non-finite values.
Results may differ from a plain program's by a relative error of at most 0.015.
Values may be sent and summed in bfloat16 or wider, within the bound.
No kernel may reach another device: no remote copies, remote signals or barrier semaphores. Data moves between devices by JAX's collectives and lax.ppermute only.
A program may use at most 448 MiB of HBM per device.

v0:
```python
from functools import partial

import jax
import jax.numpy as jnp
from jax import lax
from jax.sharding import PartitionSpec as P

MICRO = 2


EPSILON = 1e-06
MASKED = -1000000000.0


def gelu_tanh(values):
    return jax.nn.gelu(values, approximate=True)


def rms_scale(values):
    return lax.rsqrt(jnp.mean(values * values, axis=-1, keepdims=True) + EPSILON)


def norm_back(values, scale_rows, gain, grad_normed):
    scaled = grad_normed * gain
    scale_cubed = scale_rows * scale_rows * scale_rows
    return scale_rows * scaled - values * scale_cubed * jnp.mean(
        scaled * values, axis=-1, keepdims=True
    )


def gain_back(values, scale_rows, grad_normed):
    return jnp.sum(grad_normed * values * scale_rows, axis=(0, 1))


def table_probs(table_rows, live_keys):
    scores = jnp.where(live_keys[None, None, :], table_rows.astype(jnp.float32), MASKED)
    return jax.nn.softmax(scores, axis=-1)


def attend_one(mix_table, member):
    value_one, live_keys = member
    block_rows = min(512, mix_table.shape[1])

    def one_block(row_start):
        prob_block = table_probs(
            lax.dynamic_slice_in_dim(mix_table, row_start, block_rows, 1), live_keys
        )
        return jnp.einsum(
            "hqk,khd->qhd",
            prob_block.astype(jnp.bfloat16),
            value_one,
            preferred_element_type=jnp.float32,
        )

    starts = lax.iota(jnp.int32, mix_table.shape[1] // block_rows) * block_rows
    blocks = lax.map(one_block, starts)
    return blocks.reshape(value_one.shape).astype(jnp.bfloat16)


def attend_back(mix_table, table_sum, member):
    value_one, grad_one, live_keys = member
    block_rows = min(512, mix_table.shape[1])

    def block_back(inner_carry, row_start):
        table_acc, value_acc = inner_carry
        prob_block = table_probs(
            lax.dynamic_slice_in_dim(mix_table, row_start, block_rows, 1), live_keys
        )
        grad_block = lax.dynamic_slice_in_dim(grad_one, row_start, block_rows, 0)
        grad_probs = jnp.einsum(
            "qhd,khd->hqk", grad_block, value_one, preferred_element_type=jnp.float32
        )
        grad_scores = prob_block * (
            grad_probs - jnp.sum(grad_probs * prob_block, axis=-1, keepdims=True)
        )
        earlier = lax.dynamic_slice_in_dim(table_acc, row_start, block_rows, 1)
        table_acc = lax.dynamic_update_slice_in_dim(table_acc, earlier + grad_scores, row_start, 1)
        value_acc = value_acc + jnp.einsum(
            "hqk,qhd->khd",
            prob_block.astype(jnp.bfloat16),
            grad_block,
            preferred_element_type=jnp.float32,
        )
        return ((table_acc, value_acc), None)

    starts = lax.iota(jnp.int32, mix_table.shape[1] // block_rows) * block_rows
    initial = (table_sum, jnp.zeros(value_one.shape, jnp.float32))
    (table_sum, value_sum), unused = lax.scan(block_back, initial, starts)
    return (table_sum, value_sum.astype(jnp.bfloat16))


def micro_step(weights, block_in, block_grad, block_lengths, offset, feature_part):
    gain_mix, w_value, mix_table, w_out, gain_feed, w_up, w_down = weights
    seq_count = block_in.shape[0]
    seq_len = block_in.shape[1]
    heads_here = mix_table.shape[0]
    positions = lax.iota(jnp.int32, seq_len)
    live_mask = positions[None, :] < block_lengths[:, None]
    keep_rows = live_mask[:, :, None].astype(jnp.float32)
    in_float = block_in.astype(jnp.float32)
    scale_mix = rms_scale(in_float)
    mix_gain = gain_mix.astype(jnp.float32)
    feed_gain = gain_feed.astype(jnp.float32)
    normed = (in_float * scale_mix * mix_gain).astype(jnp.bfloat16)
    value_rows = jnp.dot(normed, w_value, preferred_element_type=jnp.float32).astype(jnp.bfloat16)
    value_heads = value_rows.reshape(seq_count, seq_len, heads_here, -1)
    mixed = lax.map(partial(attend_one, mix_table), (value_heads, live_mask)).reshape(
        seq_count, seq_len, -1
    )
    mix_terms = jnp.dot(mixed, w_out, preferred_element_type=jnp.float32)
    hidden = in_float + lax.psum(mix_terms.astype(jnp.bfloat16), "head").astype(jnp.float32)
    scale_feed = rms_scale(hidden)
    normed_feed = (hidden * scale_feed * feed_gain).astype(jnp.bfloat16)
    hidden_part = lax.dynamic_slice_in_dim(hidden, offset, feature_part, 2)
    up_proj = jnp.dot(normed_feed, w_up, preferred_element_type=jnp.float32)
    activated, gelu_pull = jax.vjp(gelu_tanh, up_proj)
    act_low = activated.astype(jnp.bfloat16)
    feed_out = lax.psum_scatter(
        jnp.dot(act_low, w_down, preferred_element_type=jnp.float32).astype(jnp.bfloat16),
        "head",
        scatter_dimension=2,
        tiled=True,
    ).astype(jnp.float32)
    output = (keep_rows * (hidden_part + feed_out)).astype(jnp.bfloat16)
    grad_rows = keep_rows * block_grad.astype(jnp.float32)
    grad_rows_low = grad_rows.astype(jnp.bfloat16)
    down_grad = jnp.einsum(
        "gsf,gsd->fd", act_low, grad_rows_low, preferred_element_type=jnp.float32
    )
    grad_act = jnp.einsum("gsd,fd->gsf", grad_rows_low, w_down, preferred_element_type=jnp.float32)
    grad_up_low = gelu_pull(grad_act)[0].astype(jnp.bfloat16)
    up_grad = jnp.einsum(
        "gsd,gsf->df", normed_feed, grad_up_low, preferred_element_type=jnp.float32
    )
    feed_terms = jnp.einsum("gsf,df->gsd", grad_up_low, w_up, preferred_element_type=jnp.float32)
    grad_feed_norm = lax.psum(feed_terms.astype(jnp.bfloat16), "head").astype(jnp.float32)
    gain_feed_grad = gain_back(hidden, scale_feed, grad_feed_norm)
    grad_hidden = grad_rows + norm_back(hidden, scale_feed, feed_gain, grad_feed_norm)
    grad_hidden_low = grad_hidden.astype(jnp.bfloat16)
    grad_hidden_part = lax.dynamic_slice_in_dim(grad_hidden, offset, feature_part, 2)
    projection_grad = jnp.einsum(
        "gsk,gsd->kd", mixed, grad_hidden_low, preferred_element_type=jnp.float32
    )
    grad_mixed = jnp.einsum(
        "gsd,kd->gsk", grad_hidden_low, w_out, preferred_element_type=jnp.float32
    ).astype(jnp.bfloat16)
    grad_mixed = grad_mixed.reshape(seq_count, seq_len, heads_here, -1)
    table_grad, grad_value = lax.scan(
        partial(attend_back, mix_table),
        jnp.zeros(mix_table.shape, jnp.float32),
        (value_heads, grad_mixed, live_mask),
    )
    grad_value = grad_value.reshape(seq_count, seq_len, -1)
    value_grad = jnp.einsum("gsd,gsk->dk", normed, grad_value, preferred_element_type=jnp.float32)
    norm_terms = jnp.einsum("gsk,dk->gsd", grad_value, w_value, preferred_element_type=jnp.float32)
    grad_norm = lax.psum(norm_terms.astype(jnp.bfloat16), "head").astype(jnp.float32)
    gain_mix_grad = gain_back(in_float, scale_mix, grad_norm)
    grad_input = grad_hidden_part + lax.dynamic_slice_in_dim(
        norm_back(in_float, scale_mix, mix_gain, grad_norm), offset, feature_part, 2
    )
    input_part = grad_input.astype(jnp.bfloat16)
    gradients = (
        gain_mix_grad,
        value_grad,
        table_grad,
        projection_grad,
        gain_feed_grad,
        up_grad,
        down_grad,
    )
    return (output, input_part, gradients)


def body(inputs, lengths, gain_mix, w_value, mix_table, w_out, gain_feed, w_up, w_down, out_grad):
    feature_part = inputs.shape[2]
    group_size = inputs.shape[0] // MICRO
    offset = lax.axis_index("head") * feature_part
    full_in, full_grad = (
        lax.all_gather(inputs, "head", axis=2, tiled=True),
        lax.all_gather(out_grad, "head", axis=2, tiled=True),
    )
    outputs = []
    input_parts = []
    totals = None
    for micro_index in range(MICRO):
        current = (
            lax.all_gather(gain_mix, "dp", axis=0, tiled=True),
            lax.all_gather(w_value, "dp", axis=0, tiled=True),
            lax.all_gather(mix_table, "dp", axis=1, tiled=True),
            lax.all_gather(w_out, "dp", axis=1, tiled=True),
            lax.all_gather(gain_feed, "dp", axis=0, tiled=True),
            lax.all_gather(w_up, "dp", axis=0, tiled=True),
            lax.all_gather(w_down, "dp", axis=1, tiled=True),
        )
        low_edge = micro_index * group_size
        output, input_part, gradients = micro_step(
            current,
            full_in[low_edge : low_edge + group_size],
            full_grad[low_edge : low_edge + group_size],
            lengths[low_edge : low_edge + group_size],
            offset,
            feature_part,
        )
        gradients = (
            lax.psum_scatter(gradients[0], "dp", scatter_dimension=0, tiled=True),
            lax.psum_scatter(gradients[1], "dp", scatter_dimension=0, tiled=True),
            lax.psum_scatter(gradients[2], "dp", scatter_dimension=1, tiled=True),
            lax.psum_scatter(gradients[3], "dp", scatter_dimension=1, tiled=True),
            lax.psum_scatter(gradients[4], "dp", scatter_dimension=0, tiled=True),
            lax.psum_scatter(gradients[5], "dp", scatter_dimension=0, tiled=True),
            lax.psum_scatter(gradients[6], "dp", scatter_dimension=1, tiled=True),
        )
        totals = (
            tuple(gradients) if totals is None else jax.tree.map(jnp.add, totals, tuple(gradients))
        )
        outputs.append(output)
        input_parts.append(input_part)
    return (
        jnp.concatenate(outputs, 0),
        jnp.concatenate(input_parts, 0),
        totals[0],
        totals[1],
        totals[2],
        totals[3],
        totals[4],
        totals[5],
        totals[6],
    )


def solution(mesh):
    return jax.shard_map(
        body,
        mesh=mesh,
        in_specs=(
            P("dp", None, "head"),
            P("dp"),
            P("dp"),
            P("dp", "head"),
            P("head", "dp", None),
            P("head", "dp"),
            P("dp"),
            P("dp", "head"),
            P("head", "dp"),
            P("dp", None, "head"),
        ),
        out_specs=(
            P("dp", None, "head"),
            P("dp", None, "head"),
            P("dp"),
            P("dp", "head"),
            P("head", "dp", None),
            P("head", "dp"),
            P("dp"),
            P("dp", "head"),
            P("head", "dp"),
        ),
        check_vma=False,
    )
```

profile of v0, /device:TPU:0, one launch (start us, length us, event | category | flops | bytes accessed | tf_op | source)
XLA Modules:
  0.0 2436.1 jit_solution(11937556631547163467)
XLA Ops:
  12.4 44.4 %all-reduce.5 = (bf16[768]{0:T(1024)(128)(2,1)S(1)}, bf16[768]{0:T(1024)(128)(2,1)}) all-reduce(bf16[768]{0:T(1024)(128)(2,1)S(1)} %dynamic-update-slice, bf16[768]{0:T(1024)(128)(2,1)S(1)} %dynamic-update-slice.1), channel_id=1, replica_groups=mesh['dp'=16,'head'=2] {'dp'}, use_global_device_ids=true, to_apply=%add | all-reduce | flops 1536 | bytes 6144
  58.3 43.4 %all_gather.36 = bf16[768,384]{1,0:T(8,128)(2,1)S(1)} all-gather(bf16[48,384]{1,0:T(8,128)(2,1)} %param.29), channel_id=1, replica_groups=mesh['dp'=16,'head'=2] {'dp'}, dimensions={0}, use_global_device_ids=true | all-gather | bytes 626688 | tf_op jit(solution)/shard_map/all_gather | solution.py:188
  101.7 49.8 %all_gather.38 = bf16[384,768]{0,1:T(8,128)(2,1)} all-gather(bf16[384,48]{0,1:T(8,128)(2,1)} %param.31), channel_id=1, replica_groups=mesh['dp'=16,'head'=2] {'dp'}, dimensions={1}, use_global_device_ids=true | all-gather | bytes 626688 | tf_op jit(solution)/shard_map/all_gather | solution.py:190
  162.1 36.9 %all-gather.8.cloned.1.call-done = bf16[6,1024,1024]{2,1,0:T(8,128)(2,1)} async-done(((bf16[6,64,1024]{2,1,0:T(8,128)(2,1)}), bf16[6,1024,1024]{2,1,0:T(8,128)(2,1)}) %all-gather.8.cloned.1.call-update) | async-done | bytes 12582928 | tf_op jit(solution)/shard_map/all_gather | solution.py:189
  200.4 96.6 %while.93 = (s32[]{:T(128)}, bf16[2,1024,6,64]{1,3,2,0:T(8,128)(2,1)}, pred[2,1024]{1,0:T(4,128)(4,1)}, bf16[2,1024,6,64]{1,3,2,0:T(8,128)(2,1)}, bf16[6,1024,10...) while((s32[]{:T(128)}, bf16[2,1024,6,64]{1,3,2,0:T(8,128)(2,1)}, ...), condition=%wide.region_16.17_spmd, body=%wide.region_11.16_spmd.sunk | while | flops 437257216 | bytes 102271368 | solution.py:107
  202.3 42.5 %while.99 = (s32[]{:T(128)}, bf16[2,512,6,64]{1,3,2,0:T(8,128)(2,1)S(1)}, pred[1024]{0:T(1024)(128)(4,1)S(1)}, s32[2]{0:T(128)S(1)}, bf16[6,1024,1024]{2,1,0:T(8...) while((s32[]{:T(128)}, bf16[2,512,6,64]{1,3,2,0:T(8,128)(2,1)S(1)}, ...), condition=%wide.region_15.15_spmd, body=%wide.region_12.14_spmd.sunk | while | flops 437257216 | bytes 95977656 | solution.py:56
  250.6 42.5 %while.99 = (s32[]{:T(128)}, bf16[2,512,6,64]{1,3,2,0:T(8,128)(2,1)S(1)}, pred[1024]{0:T(1024)(128)(4,1)S(1)}, s32[2]{0:T(128)S(1)}, bf16[6,1024,1024]{2,1,0:T(8...) while((s32[]{:T(128)}, bf16[2,512,6,64]{1,3,2,0:T(8,128)(2,1)S(1)}, ...), condition=%wide.region_15.15_spmd, body=%wide.region_12.14_spmd.sunk | while | flops 437257216 | bytes 95977656 | solution.py:56
  298.3 96.9 %while.91 = (s32[]{:T(128)}, bf16[2,1024,6,64]{1,3,2,0:T(8,128)(2,1)}, pred[2,1024]{1,0:T(4,128)(4,1)}, bf16[2,1024,6,64]{1,3,2,0:T(8,128)(2,1)}, bf16[6,1024,10...) while((s32[]{:T(128)}, bf16[2,1024,6,64]{1,3,2,0:T(8,128)(2,1)}, ...), condition=%wide.region_6.7_spmd, body=%wide.region_1.6_spmd.sunk | while | flops 437257216 | bytes 102271368 | solution.py:107
  300.6 42.5 %while.98 = (s32[]{:T(128)}, bf16[2,512,6,64]{1,3,2,0:T(8,128)(2,1)S(1)}, pred[1024]{0:T(1024)(128)(4,1)S(1)}, s32[2]{0:T(128)S(1)}, bf16[6,1024,1024]{2,1,0:T(8...) while((s32[]{:T(128)}, bf16[2,512,6,64]{1,3,2,0:T(8,128)(2,1)S(1)}, ...), condition=%wide.region_5.5_spmd, body=%wide.region_2.4_spmd.sunk | while | flops 437257216 | bytes 95977656 | solution.py:56
  348.9 42.5 %while.98 = (s32[]{:T(128)}, bf16[2,512,6,64]{1,3,2,0:T(8,128)(2,1)S(1)}, pred[1024]{0:T(1024)(128)(4,1)S(1)}, s32[2]{0:T(128)S(1)}, bf16[6,1024,1024]{2,1,0:T(8...) while((s32[]{:T(128)}, bf16[2,512,6,64]{1,3,2,0:T(8,128)(2,1)S(1)}, ...), condition=%wide.region_5.5_spmd, body=%wide.region_2.4_spmd.sunk | while | flops 437257216 | bytes 95977656 | solution.py:56
  407.0 29.3 %all-reduce.17.cloned.1.call-done = (bf16[2,1024,768]{2,1,0:T(8,128)(2,1)}, bf16[2,1024,768]{2,1,0:T(8,128)(2,1)}) async-done(((bf16[2,1024,768]{2,1,0:T(8,128)(2,1)}, bf16[2,1024,768]{2,1,0:T(8,128)(2,1)}), (bf16[2,1024,768]{2,1,0:T(8,128)(2,1)}, bf16[2,1024,768]{2,1,0:T(8,128)(2,1)})) %all-reduce.17.cloned.1.call-update) | async-done | bytes 6291472 | tf_op jit(solution)/shard_map/psum | solution.py:111
  442.3 60.6 %all-gather.10.cloned.1.call-done = bf16[768,1536]{1,0:T(8,128)(2,1)} async-done(((bf16[48,1536]{1,0:T(8,128)(2,1)}), bf16[768,1536]{1,0:T(8,128)(2,1)}) %all-gather.10.cloned.1.call-update) | async-done | bytes 2359312 | tf_op jit(solution)/shard_map/all_gather | solution.py:192
  513.6 53.4 %all-gather.12.cloned.1.call-done = bf16[1536,768]{0,1:T(8,128)(2,1)} async-done(((bf16[1536,48]{0,1:T(8,128)(2,1)}), bf16[1536,768]{0,1:T(8,128)(2,1)}) %all-gather.12.cloned.1.call-update) | async-done | bytes 2359312 | tf_op jit(solution)/shard_map/all_gather | solution.py:193
  731.3 364.2 %while.97 = (s32[]{:T(128)}, f32[6,1024,1024]{2,1,0:T(8,128)}, bf16[2,1024,6,64]{1,3,2,0:T(8,128)(2,1)}, pred[2,1024]{1,0:T(4,128)(4,1)}, bf16[2,1024,6,64]{1,3,...) while((s32[]{:T(128)}, f32[6,1024,1024]{2,1,0:T(8,128)}, ...), condition=%wide.region_39.40_spmd, body=%wide.region_33.39_spmd.sunk | while | flops 1281496064 | bytes 219094976 | solution.py:148
  733.7 178.6 %while.101 = (s32[]{:T(128)}, f32[6,1024,1024]{2,1,0:T(8,128)}, f32[1024,6,64]{0,2,1:T(8,128)S(1)}, s32[2]{0:T(128)S(1)}, pred[1024]{0:T(1024)(128)(4,1)S(1)}, /...) while((s32[]{:T(128)}, f32[6,1024,1024]{2,1,0:T(8,128)}, ...), condition=%wide.region_38.38_spmd.clone, body=%wide.region_34.37_spmd.clone.sunk | while | flops 1281102848 | bytes 213587664 | solution.py:88
  788.8 34.6 %dynamic_update_slice.46 = f32[6,1024,1024]{2,1,0:T(8,128)} dynamic-update-slice(f32[6,1024,1024]{2,1,0:T(8,128)} %get-tuple-element.977, f32[6,512,1024]{2,1,0:T(8,128)} %multiply_add_fusion.4, s32[]{:T(128)} %constant.146.clone.1..sunk.7..sunk, s32[]{:T(128)S(6)} %select_n.147, s32[]{:T(128)} %constant.146.clone.1..sunk.7..sunk) | dynamic-update-slice | bytes 25165828 | tf_op jit(solution)/shard_map/while/body/eval_jaxpr/while/body/eval_jaxpr/dynamic_update_slice | solution.py:77
  878.3 34.1 %dynamic_update_slice.46 = f32[6,1024,1024]{2,1,0:T(8,128)} dynamic-update-slice(f32[6,1024,1024]{2,1,0:T(8,128)} %get-tuple-element.977, f32[6,512,1024]{2,1,0:T(8,128)} %multiply_add_fusion.4, s32[]{:T(128)} %constant.146.clone.1..sunk.7..sunk, s32[]{:T(128)S(6)} %select_n.147, s32[]{:T(128)} %constant.146.clone.1..sunk.7..sunk) | dynamic-update-slice | bytes 25165828 | tf_op jit(solution)/shard_map/while/body/eval_jaxpr/while/body/eval_jaxpr/dynamic_update_slice | solution.py:77
  915.7 178.6 %while.101 = (s32[]{:T(128)}, f32[6,1024,1024]{2,1,0:T(8,128)}, f32[1024,6,64]{0,2,1:T(8,128)S(1)}, s32[2]{0:T(128)S(1)}, pred[1024]{0:T(1024)(128)(4,1)S(1)}, /...) while((s32[]{:T(128)}, f32[6,1024,1024]{2,1,0:T(8,128)}, ...), condition=%wide.region_38.38_spmd.clone, body=%wide.region_34.37_spmd.clone.sunk | while | flops 1281102848 | bytes 213587664 | solution.py:88
  970.7 34.6 %dynamic_update_slice.46 = f32[6,1024,1024]{2,1,0:T(8,128)} dynamic-update-slice(f32[6,1024,1024]{2,1,0:T(8,128)} %get-tuple-element.977, f32[6,512,1024]{2,1,0:T(8,128)} %multiply_add_fusion.4, s32[]{:T(128)} %constant.146.clone.1..sunk.7..sunk, s32[]{:T(128)S(6)} %select_n.147, s32[]{:T(128)} %constant.146.clone.1..sunk.7..sunk) | dynamic-update-slice | bytes 25165828 | tf_op jit(solution)/shard_map/while/body/eval_jaxpr/while/body/eval_jaxpr/dynamic_update_slice | solution.py:77
  1060.2 34.1 %dynamic_update_slice.46 = f32[6,1024,1024]{2,1,0:T(8,128)} dynamic-update-slice(f32[6,1024,1024]{2,1,0:T(8,128)} %get-tuple-element.977, f32[6,512,1024]{2,1,0:T(8,128)} %multiply_add_fusion.4, s32[]{:T(128)} %constant.146.clone.1..sunk.7..sunk, s32[]{:T(128)S(6)} %select_n.147, s32[]{:T(128)} %constant.146.clone.1..sunk.7..sunk) | dynamic-update-slice | bytes 25165828 | tf_op jit(solution)/shard_map/while/body/eval_jaxpr/while/body/eval_jaxpr/dynamic_update_slice | solution.py:77
  1108.4 365.0 %while.95 = (s32[]{:T(128)}, f32[6,1024,1024]{2,1,0:T(8,128)}, bf16[2,1024,6,64]{1,3,2,0:T(8,128)(2,1)}, pred[2,1024]{1,0:T(4,128)(4,1)}, bf16[2,1024,6,64]{1,3,...) while((s32[]{:T(128)}, f32[6,1024,1024]{2,1,0:T(8,128)}, ...), condition=%wide.region_28.29_spmd, body=%wide.region_22.28_spmd.sunk | while | flops 1281496064 | bytes 219094976 | solution.py:148
  1110.7 179.0 %while.100 = (s32[]{:T(128)}, f32[6,1024,1024]{2,1,0:T(8,128)}, f32[1024,6,64]{0,2,1:T(8,128)S(1)}, s32[2]{0:T(128)S(1)}, pred[1024]{0:T(1024)(128)(4,1)S(1)}, /...) while((s32[]{:T(128)}, f32[6,1024,1024]{2,1,0:T(8,128)}, ...), condition=%wide.region_27.27_spmd.clone, body=%wide.region_23.26_spmd.clone.sunk | while | flops 1281102848 | bytes 213587664 | solution.py:88
  1166.0 34.6 %dynamic_update_slice.47 = f32[6,1024,1024]{2,1,0:T(8,128)} dynamic-update-slice(f32[6,1024,1024]{2,1,0:T(8,128)} %get-tuple-element.1010, f32[6,512,1024]{2,1,0:T(8,128)} %multiply_add_fusion.5, s32[]{:T(128)} %constant.146.clone.1..sunk.5..sunk, s32[]{:T(128)S(6)} %select_n.153, s32[]{:T(128)} %constant.146.clone.1..sunk.5..sunk) | dynamic-update-slice | bytes 25165828 | tf_op jit(solution)/shard_map/while/body/eval_jaxpr/while/body/eval_jaxpr/dynamic_update_slice | solution.py:77
  1255.6 34.1 %dynamic_update_slice.47 = f32[6,1024,1024]{2,1,0:T(8,128)} dynamic-update-slice(f32[6,1024,1024]{2,1,0:T(8,128)} %get-tuple-element.1010, f32[6,512,1024]{2,1,0:T(8,128)} %multiply_add_fusion.5, s32[]{:T(128)} %constant.146.clone.1..sunk.5..sunk, s32[]{:T(128)S(6)} %select_n.153, s32[]{:T(128)} %constant.146.clone.1..sunk.5..sunk) | dynamic-update-slice | bytes 25165828 | tf_op jit(solution)/shard_map/while/body/eval_jaxpr/while/body/eval_jaxpr/dynamic_update_slice | solution.py:77
  1293.0 179.0 %while.100 = (s32[]{:T(128)}, f32[6,1024,1024]{2,1,0:T(8,128)}, f32[1024,6,64]{0,2,1:T(8,128)S(1)}, s32[2]{0:T(128)S(1)}, pred[1024]{0:T(1024)(128)(4,1)S(1)}, /...) while((s32[]{:T(128)}, f32[6,1024,1024]{2,1,0:T(8,128)}, ...), condition=%wide.region_27.27_spmd.clone, body=%wide.region_23.26_spmd.clone.sunk | while | flops 1281102848 | bytes 213587664 | solution.py:88
  1348.2 34.6 %dynamic_update_slice.47 = f32[6,1024,1024]{2,1,0:T(8,128)} dynamic-update-slice(f32[6,1024,1024]{2,1,0:T(8,128)} %get-tuple-element.1010, f32[6,512,1024]{2,1,0:T(8,128)} %multiply_add_fusion.5, s32[]{:T(128)} %constant.146.clone.1..sunk.5..sunk, s32[]{:T(128)S(6)} %select_n.153, s32[]{:T(128)} %constant.146.clone.1..sunk.5..sunk) | dynamic-update-slice | bytes 25165828 | tf_op jit(solution)/shard_map/while/body/eval_jaxpr/while/body/eval_jaxpr/dynamic_update_slice | solution.py:77
  1437.9 34.1 %dynamic_update_slice.47 = f32[6,1024,1024]{2,1,0:T(8,128)} dynamic-update-slice(f32[6,1024,1024]{2,1,0:T(8,128)} %get-tuple-element.1010, f32[6,512,1024]{2,1,0:T(8,128)} %multiply_add_fusion.5, s32[]{:T(128)} %constant.146.clone.1..sunk.5..sunk, s32[]{:T(128)S(6)} %select_n.153, s32[]{:T(128)} %constant.146.clone.1..sunk.5..sunk) | dynamic-update-slice | bytes 25165828 | tf_op jit(solution)/shard_map/while/body/eval_jaxpr/while/body/eval_jaxpr/dynamic_update_slice | solution.py:77
  1615.6 42.6 %all-reduce.4 = (f32[768]{0:T(1024)S(1)}, f32[768]{0:T(1024)S(1)}) all-reduce(f32[768]{0:T(1024)S(1)} %add.233, f32[768]{0:T(1024)S(1)} %add.237), channel_id=11, replica_groups=mesh['dp'=16,'head'=2] {'dp'}, use_global_device_ids=true, to_apply=%region_43.44.clone | all-reduce | flops 1536 | bytes 12288
  1669.8 106.5 %reduce-scatter.12.cloned.1.call-done = f32[48,384]{1,0:T(8,128)} async-done(((f32[768,384]{1,0:T(8,128)}), f32[48,384]{1,0:T(8,128)}) %reduce-scatter.12.cloned.1.call-update) | async-done | bytes 73744 | tf_op jit(solution)/shard_map/reduce_scatter | solution.py:206
  1776.3 143.1 %reduce-scatter.20.cloned.1.call-done = f32[1536,48]{0,1:T(8,128)} async-done(((f32[1536,768]{0,1:T(8,128)}), f32[1536,48]{0,1:T(8,128)}) %reduce-scatter.20.cloned.1.call-update) | async-done | bytes 294928 | tf_op jit(solution)/shard_map/reduce_scatter | solution.py:211
  1919.4 141.4 %reduce-scatter.18.cloned.1.call-done = f32[48,1536]{1,0:T(8,128)} async-done(((f32[768,1536]{1,0:T(8,128)}), f32[48,1536]{1,0:T(8,128)}) %reduce-scatter.18.cloned.1.call-update) | async-done | bytes 294928 | tf_op jit(solution)/shard_map/reduce_scatter | solution.py:210
  2060.7 368.4 %reduce-scatter.14.cloned.1.call-done = f32[6,64,1024]{2,1,0:T(8,128)} async-done(((f32[6,1024,1024]{2,1,0:T(8,128)}), f32[6,64,1024]{2,1,0:T(8,128)}) %reduce-scatter.14.cloned.1.call-update) | async-done | bytes 1572880 | tf_op jit(solution)/shard_map/reduce_scatter | solution.py:207
  (347 shorter events, 992.0 us)
Async XLA Ops:
  7.2 144.3 %all-gather.6.cloned.1.call-start = ((), (), s32[]{:S(2)}) async-start(), calls=%async_computation.7 | async-start | bytes 9437184 | tf_op jit(solution)/shard_map/all_gather | solution.py:179
  7.9 191.1 %all-gather.8.cloned.1.call-start = ((), (), s32[]{:S(2)}) async-start(), calls=%async_computation.8 | async-start | bytes 13369344 | tf_op jit(solution)/shard_map/all_gather | solution.py:189
  8.7 427.6 %all-reduce.17.cloned.1.call-start = ((), (), s32[]{:S(2)}) async-start(), calls=%async_computation.21 | async-start | bytes 12582912 | tf_op jit(solution)/shard_map/psum | solution.py:111
  56.8 102.4 %copy-start.33 = (f32[768]{0:T(1024)}, f32[768]{0:T(1024)S(1)}, u32[]{:S(2)}) copy-start(f32[768]{0:T(1024)S(1)} %convert_element_type.202) | copy-start | bytes 9220
  101.7 57.6 %copy-start.14 = (bf16[768,384]{1,0:T(8,128)(2,1)}, bf16[768,384]{1,0:T(8,128)(2,1)S(1)}, u32[]{:S(2)}) copy-start(bf16[768,384]{1,0:T(8,128)(2,1)S(1)} %all_gather.36) | copy-start | bytes 1769476
  298.3 97.0 %copy-start.10 = (bf16[384,768]{0,1:T(8,128)(2,1)S(1)}, bf16[384,768]{0,1:T(8,128)(2,1)}, u32[]{:S(2)}) copy-start(bf16[384,768]{0,1:T(8,128)(2,1)} %all_gather.38) | copy-start | bytes 1769476
  405.1 97.7 %all-gather.10.cloned.1.call-start = ((), (), s32[]{:S(2)}) async-start(), calls=%async_computation.9 | async-start | bytes 2506752 | tf_op jit(solution)/shard_map/all_gather | solution.py:192
  405.7 161.3 %all-gather.12.cloned.1.call-start = ((), (), s32[]{:S(2)}) async-start(), calls=%async_computation.10 | async-start | bytes 2506752 | tf_op jit(solution)/shard_map/all_gather | solution.py:193
  406.3 177.6 %all-gather.14.cloned.1.call-start = ((), (), s32[]{:S(2)}) async-start(), calls=%async_computation.11 | async-start | bytes 9437184 | tf_op jit(solution)/shard_map/all_gather | solution.py:180
  406.9 281.5 %all-reduce.15.cloned.1.call-start = ((), (), s32[]{:S(2)}) async-start(), calls=%async_computation.20 | async-start | bytes 12582912 | tf_op jit(solution)/shard_map/psum | solution.py:136
  407.0 292.4 %copy-start.27 = (f32[768]{0:T(1024)}, f32[768]{0:T(1024)S(1)}, u32[]{:S(2)}) copy-start(f32[768]{0:T(1024)S(1)} %convert_element_type.207) | copy-start | bytes 9220
  442.2 257.1 %copy-start.15 = (f32[2,1024]{1,0:T(2,128)}, f32[2,1024]{1,0:T(2,128)S(1)}, u32[]{:S(2)}) copy-start(f32[2,1024]{1,0:T(2,128)S(1)} %get-tuple-element.534) | copy-start | bytes 24580
  442.2 257.1 %copy-start.17 = (f32[2,1024]{1,0:T(2,128)}, f32[2,1024]{1,0:T(2,128)S(1)}, u32[]{:S(2)}) copy-start(f32[2,1024]{1,0:T(2,128)S(1)} %get-tuple-element.536) | copy-start | bytes 24580
  502.8 81.1 %copy-start.23 = (f32[2,1024]{1,0:T(2,128)S(1)}, f32[2,1024]{1,0:T(2,128)}, u32[]{:S(2)}) copy-start(f32[2,1024]{1,0:T(2,128)} %get-tuple-element.546) | copy-start | bytes 24580
  502.8 107.7 %slice-start = ((s8[6291456]{0:T(1024)(128)(4,1)}), s8[2097152]{0:T(1024)(128)(4,1)S(1)}, s32[]{:S(2)}) async-start(s8[6291456]{0:T(1024)(128)(4,1)} %bitcast.182), calls=%async_computation.22 | async-start | bytes 4194304
  583.9 17.2 copy-start.42
  583.9 26.6 %slice-start.1 = ((s8[6291456]{0:T(1024)(128)(4,1)}), s8[4194304]{0:T(1024)(128)(4,1)S(1)}, s32[]{:S(2)}) async-start(s8[6291456]{0:T(1024)(128)(4,1)} %bitcast.182), calls=%async_computation.23 | async-start | bytes 8388608
  601.1 17.6 slice-start.4
  641.5 945.4 %reduce-scatter.24.cloned.1.call-start = ((), (), s32[]{:S(2)}) async-start(), calls=%async_computation.18 | async-start | bytes 4718592
  664.9 926.5 %reduce-scatter.22.cloned.1.call-start = ((), (), s32[]{:S(2)}) async-start(), calls=%async_computation.17 | async-start | bytes 4718592
  683.2 16.1 slice-start.2
  688.4 916.1 %all-reduce.13.cloned.1.call-start = ((), (), s32[]{:S(2)}) async-start(), calls=%async_computation.19 | async-start | bytes 12582912 | tf_op jit(solution)/shard_map/psum | solution.py:156
  1483.6 186.2 %reduce-scatter.16.cloned.1.call-start = ((), (), s32[]{:S(2)}) async-start(), calls=%async_computation.14 | async-start | bytes 1253376 | tf_op jit(solution)/shard_map/reduce_scatter | solution.py:208
  1494.4 13.9 copy-start.12
  1494.4 13.9 copy-start.22
  1494.5 13.9 copy-start.34
  1494.5 281.8 %reduce-scatter.12.cloned.1.call-start = ((), (), s32[]{:S(2)}) async-start(), calls=%async_computation.12 | async-start | bytes 1253376 | tf_op jit(solution)/shard_map/reduce_scatter | solution.py:206
  1518.7 400.7 %reduce-scatter.20.cloned.1.call-start = ((), (), s32[]{:S(2)}) async-start(), calls=%async_computation.16 | async-start | bytes 5013504 | tf_op jit(solution)/shard_map/reduce_scatter | solution.py:211
  1531.8 529.0 %reduce-scatter.18.cloned.1.call-start = ((), (), s32[]{:S(2)}) async-start(), calls=%async_computation.15 | async-start | bytes 5013504 | tf_op jit(solution)/shard_map/reduce_scatter | solution.py:210
  1552.3 876.8 %reduce-scatter.14.cloned.1.call-start = ((), (), s32[]{:S(2)}) async-start(), calls=%async_computation.13 | async-start | bytes 26738688 | tf_op jit(solution)/shard_map/reduce_scatter | solution.py:207
  1604.5 54.9 %copy-start.30 = (f32[2,1024]{1,0:T(2,128)S(1)}, f32[2,1024]{1,0:T(2,128)}, u32[]{:S(2)}) copy-start(f32[2,1024]{1,0:T(2,128)} %get-tuple-element.548) | copy-start | bytes 24580
  1615.6 48.7 %copy-start.29 = (f32[2,1024]{1,0:T(2,128)S(1)}, f32[2,1024]{1,0:T(2,128)}, u32[]{:S(2)}) copy-start(f32[2,1024]{1,0:T(2,128)} %get-tuple-element.531) | copy-start | bytes 24580
  (45 other events, 398.1 us)
Sparse Core Ops, SparseCore 0:
  9.6 19.2 all-gather.5
  31.6 167.3 all-gather.7
  405.3 30.9 all-reduce.16
  439.3 63.4 all-gather.9
  505.9 61.0 all-gather.11
  568.5 15.3 all-gather.13
  641.7 33.3 all-reduce.14
  677.9 12.0 reduce-scatter.23
  692.3 12.0 reduce-scatter.21
  1483.7 33.2 all-reduce.12
  1523.1 124.5 reduce-scatter.15
  1653.6 122.6 reduce-scatter.11
  1782.9 136.4 reduce-scatter.19
  1925.0 135.7 reduce-scatter.17
  2067.9 361.2 reduce-scatter.13
where the time goes:
time: 2450 us; the launch traced here: 2440 us
  waiting for transfers between devices  960 us (39%)
  matrix products  571 us (23%)
  local copies, waits for them, and re-layouts  387 us (16%)
  other arithmetic  288 us (12%)
  blocking collectives  180 us (7%)
  loops' own time  33.3 us (1%)
    reduce_scatter x1, waiting for transfers between devices, body(): lax.psum_scatter(gradients[2], 'dp', scatter_dimension=1, tiled=True)  368 us
    dynamic_update_slice x8, local copies, waits for them, and re-layouts, block_back(): lax.dynamic_update_slice_in_dim(table_acc, earlier + grad_scores, row_sta...  275 us
    sub x16, other arithmetic, table_probs(): return jax.nn.softmax(scores, axis=-1)  187 us
    dot_general x8, matrix products, block_back(): jnp.einsum('qhd,khd->hqk', grad_block, value_one, preferred_element_type=...  171 us
    reduce_scatter x1, waiting for transfers between devices, body(): lax.psum_scatter(gradients[6], 'dp', scatter_dimension=1, tiled=True)  143 us
    reduce_scatter x1, waiting for transfers between devices, body(): lax.psum_scatter(gradients[5], 'dp', scatter_dimension=0, tiled=True)  141 us
    reduce_scatter x1, waiting for transfers between devices, body(): lax.psum_scatter(gradients[1], 'dp', scatter_dimension=0, tiled=True)  106 us
    sub x8, matrix products, block_back(): grad_probs - jnp.sum(grad_probs * prob_block, axis=-1, keepdims=True)  94.6 us
  transfers between devices with their start and end apart: 15, of which 9 were waited for; matrix products, arithmetic and copies ran while one was open for 41% of the time, Pallas kernels for 0%

commit v1 on v0

v1 whole, which is shorter than its diff:
```python
from functools import partial

import jax
import jax.numpy as jnp
from jax import lax
from jax.experimental import pallas as pl
from jax.experimental.pallas import tpu as pltpu
from jax.sharding import PartitionSpec as P

EPSILON = 1e-06
GELU_C = 0.7978845608028654
GELU_K = 0.044715
PLANE = 4
HEAD_DIM = 64
VMEM = 56 * 1024 * 1024

BF16 = jnp.bfloat16
F32 = jnp.float32


def dot_nt(a, b):
    return lax.dot_general(a, b, (((1,), (1,)), ((), ())), preferred_element_type=F32)


def dot_tn(a, b):
    return lax.dot_general(a, b, (((0,), (0,)), ((), ())), preferred_element_type=F32)


def dot_nn(a, b):
    return jnp.dot(a, b, preferred_element_type=F32)


def mix_forward_kernel(core, ta, tb, v0, v1, v2, v3, masks, o0, o1, o2, o3, inv_out, e_out):
    first = core[0] == 0
    rows = ta.shape[0] * ta.shape[2]
    half = ta.shape[3]
    ea = jnp.exp(ta[:, 0].reshape(rows, half).astype(F32)).astype(BF16)
    eb = jnp.exp(tb[:, 0].reshape(rows, half).astype(F32)).astype(BF16)
    weights = jnp.concatenate([jnp.where(first, ea, eb), jnp.where(first, eb, ea)], axis=1)
    e_out[0] = weights
    seq = weights.shape[1]
    values = jnp.concatenate([v[:, 0].reshape(-1, seq) for v in (v0, v1, v2, v3)], axis=0)
    totals = dot_nt(masks[...], weights)[:8]
    inverse = 1.0 / totals
    inv_out[0] = inverse
    mixed = dot_nt(values, weights)
    for k, out in enumerate((o0, o1, o2, o3)):
        for s in range(2):
            item = 2 * k + s
            part = mixed[item * HEAD_DIM : (item + 1) * HEAD_DIM] * inverse[item : item + 1]
            out[s, 0] = part.astype(BF16)


def mix_backward_kernel(
    core, e, v0, v1, v2, v3, g0, g1, g2, g3, x0, x1, x2, x3, inv, masks,
    keep, send, w0, w1, w2, w3, total,
):
    step = pl.program_id(1)
    first = core[0] == 0
    rows = e.shape[1]
    seq = e.shape[2]
    half = seq // 2
    weights = e[0]
    scaled = []
    offsets = []
    for grad, mixed in ((g0, x0), (g1, x1), (g2, x2), (g3, x3)):
        for s in range(2):
            item = len(scaled)
            inverse = inv[0, item : item + 1]
            part = grad[s, 0].astype(F32)
            offsets.append(
                -jnp.sum(part * mixed[s, 0].astype(F32), axis=0, keepdims=True) * inverse
            )
            scaled.append((part * inverse).astype(BF16))
    offsets.append(jnp.zeros((8, rows), F32))
    scaled = jnp.concatenate(scaled, axis=0)
    offset_rows = jnp.concatenate(offsets, axis=0).astype(BF16)
    values = jnp.concatenate([v[:, 0].reshape(-1, seq) for v in (v0, v1, v2, v3)], axis=0)

    @pl.when(step == 0)
    def _():
        total[...] = jnp.zeros_like(total)

    total[...] += dot_nn(scaled, weights)
    scores = dot_tn(scaled, values) + dot_tn(offset_rows, masks[...])
    scores = weights.astype(F32) * scores
    low = scores[:, :half].astype(BF16)
    high = scores[:, half:].astype(BF16)
    shape = keep.shape[0], keep.shape[2], half
    keep[:, 0] = jnp.where(first, low, high).reshape(shape)
    send[:, 0] = jnp.where(first, high, low).reshape(shape)

    @pl.when(step == pl.num_programs(1) - 1)
    def _():
        for k, out in enumerate((w0, w1, w2, w3)):
            for s in range(2):
                item = 2 * k + s
                live = masks[item : item + 1].astype(F32)
                part = total[item * HEAD_DIM : (item + 1) * HEAD_DIM] * live
                out[s, 0] = part.astype(BF16)


def mixing_specs(blocks, block_rows, seq):
    group = max(1, 256 // block_rows)
    rows = group * block_rows
    steps = blocks // group
    half = seq // 2
    table = pl.BlockSpec((group, 1, block_rows, half), lambda h, i, c: (i, h, 0, 0))
    whole = pl.BlockSpec((2, 1, HEAD_DIM, seq), lambda h, i, c: (0, h, 0, 0))
    tokens = pl.BlockSpec((2, 1, HEAD_DIM, rows), lambda h, i, c: (0, h, 0, i))
    inverse = pl.BlockSpec((1, 8, rows), lambda h, i, c: (h, 0, i))
    expo = pl.BlockSpec((1, rows, seq), lambda h, i, c: (h, i, 0))
    masks = pl.BlockSpec((16, seq), lambda h, i, c: (0, 0))
    return steps, table, whole, tokens, inverse, expo, masks


def mix_forward(core, tab_a, tab_b, values, masks):
    blocks, heads, block_rows, half = tab_a.shape
    seq = 2 * half
    steps, table, whole, tokens, inverse, expo, mask = mixing_specs(blocks, block_rows, seq)
    piece = jax.ShapeDtypeStruct(values[0].shape, BF16)
    outs = pl.pallas_call(
        mix_forward_kernel,
        grid_spec=pltpu.PrefetchScalarGridSpec(
            num_scalar_prefetch=1,
            grid=(heads, steps),
            in_specs=[table, table] + [whole] * 4 + [mask],
            out_specs=[tokens] * 4 + [inverse, expo],
        ),
        out_shape=[piece] * 4
        + [
            jax.ShapeDtypeStruct((heads, 8, seq), F32),
            jax.ShapeDtypeStruct((heads, seq, seq), BF16),
        ],
        compiler_params=pltpu.CompilerParams(vmem_limit_bytes=VMEM),
        cost_estimate=pl.CostEstimate(
            flops=2 * heads * seq * seq * 520,
            bytes_accessed=heads * seq * seq * 4,
            transcendentals=heads * seq * seq,
        ),
    )(core, tab_a, tab_b, *values, masks)
    return outs[:4], outs[4], outs[5]


def mix_backward(core, expo_table, values, grads, mixed, inverse_sums, masks, blocks):
    heads, seq = expo_table.shape[:2]
    block_rows = seq // blocks
    half = seq // 2
    steps, table, whole, tokens, inverse, expo, mask = mixing_specs(blocks, block_rows, seq)
    piece = jax.ShapeDtypeStruct(values[0].shape, BF16)
    part = jax.ShapeDtypeStruct((blocks, heads, block_rows, half), BF16)
    outs = pl.pallas_call(
        mix_backward_kernel,
        grid_spec=pltpu.PrefetchScalarGridSpec(
            num_scalar_prefetch=1,
            grid=(heads, steps),
            in_specs=[expo] + [whole] * 4 + [tokens] * 8 + [inverse, mask],
            out_specs=[table, table] + [whole] * 4,
            scratch_shapes=[pltpu.VMEM((8 * HEAD_DIM, seq), F32)],
        ),
        out_shape=[part, part] + [piece] * 4,
        compiler_params=pltpu.CompilerParams(vmem_limit_bytes=VMEM),
        cost_estimate=pl.CostEstimate(
            flops=4 * heads * seq * seq * 520,
            bytes_accessed=heads * seq * seq * 4,
            transcendentals=0,
        ),
    )(core, expo_table, *values, *grads, *mixed, inverse_sums, masks)
    return outs[0], outs[1], outs[2:]


def feed_kernel(
    lens, hidden, grad, gain, up_a, up_b, down_a, down_b,
    out, grad_hidden, grad_low, act, grad_up, normed, gain_sum,
):
    step = pl.program_id(0)
    rows = hidden.shape[0]
    width = up_a.shape[1]
    per_item = pl.num_programs(0) // 2
    h = hidden[...]
    gains = gain[...]
    scale = lax.rsqrt(jnp.mean(h * h, axis=-1, keepdims=True) + EPSILON)
    n = (h * scale * gains).astype(BF16)
    normed[...] = n
    g = grad[...]
    feed = jnp.zeros(h.shape, F32)
    back = jnp.zeros(h.shape, F32)
    chunk = 512
    for part, (up, down) in enumerate(((up_a, down_a), (up_b, down_b))):
        for start in range(0, width, chunk):
            w_up = up[:, start : start + chunk]
            w_down = down[:, start : start + chunk]
            u = dot_nn(n, w_up)
            ga = dot_nn(g, w_down)
            square = u * u
            t = jnp.tanh(u * (GELU_C + GELU_C * GELU_K * square))
            low = 0.5 + 0.5 * t
            a = (u * low).astype(BF16)
            slope = low + (0.5 * u) * (1.0 - t * t) * (GELU_C + 3.0 * GELU_C * GELU_K * square)
            gu = (slope * ga).astype(BF16)
            where = slice(part * width + start, part * width + start + chunk)
            act[:, where] = a
            grad_up[:, where] = gu
            feed += dot_nt(a, w_down)
            back += dot_nt(gu, w_up)
    item = step // per_item
    first = (step % per_item) * rows
    position = first + lax.broadcasted_iota(jnp.int32, (rows, 1), 0)
    live = (position < lens[item]).astype(F32)
    out[...] = (live * (h + feed)).astype(BF16)
    q = back * gains
    gh = (
        g.astype(F32)
        + scale * q
        - h * (scale * scale * scale) * jnp.mean(q * h, axis=-1, keepdims=True)
    )
    grad_hidden[...] = gh
    grad_low[...] = gh.astype(BF16)
    terms = jnp.sum((back * h * scale).reshape(rows // 8, 8, -1), axis=0)

    @pl.when(step == 0)
    def _():
        gain_sum[...] = jnp.zeros_like(gain_sum)

    gain_sum[...] += terms


def feed(lens, hidden, grad, gain, up, down):
    tokens, features = hidden.shape
    width = up[0].shape[1]
    rows = 256
    steps = tokens // rows
    row = lambda n: pl.BlockSpec((rows, n), lambda i, c: (i, 0))
    fixed = lambda shape: pl.BlockSpec(shape, lambda i, c: (0, 0), pipeline_mode=pl.Buffered(1))
    shape = lambda n, d: jax.ShapeDtypeStruct((tokens, n), d)
    return pl.pallas_call(
        feed_kernel,
        grid_spec=pltpu.PrefetchScalarGridSpec(
            num_scalar_prefetch=1,
            grid=(steps,),
            in_specs=[row(features), row(features), fixed((1, features))]
            + [fixed((features, width))] * 4,
            out_specs=[
                row(features),
                row(features),
                row(features),
                row(2 * width),
                row(2 * width),
                row(features),
                pl.BlockSpec((8, features), lambda i, c: (0, 0)),
            ],
        ),
        out_shape=[
            shape(features, BF16),
            shape(features, F32),
            shape(features, BF16),
            shape(2 * width, BF16),
            shape(2 * width, BF16),
            shape(features, BF16),
            jax.ShapeDtypeStruct((8, features), F32),
        ],
        compiler_params=pltpu.CompilerParams(vmem_limit_bytes=VMEM),
        cost_estimate=pl.CostEstimate(
            flops=2 * 4 * tokens * features * 2 * width,
            bytes_accessed=tokens * (features * 16 + 8 * width) + features * width * 8,
            transcendentals=tokens * 2 * width,
        ),
    )(lens, hidden, grad, gain, *up, *down)


def body(inputs, lengths, gain_mix, w_value, mix_table, w_out, gain_feed, w_up, w_down, out_grad):
    ranks = lax.axis_size("dp")
    blocks = ranks // PLANE
    rank = lax.axis_index("dp")
    core = lax.axis_index("head")
    place = rank % PLANE
    items, seq, feature_part = inputs.shape
    mine = items // 2
    features = 2 * feature_part
    first = core == 0
    core_ref = core.astype(jnp.int32).reshape(1)
    lines = [[b * PLANE + q for b in range(blocks)] for q in range(PLANE)]

    def sibling(t):
        return lax.ppermute(t, "head", [(0, 1), (1, 0)])

    def plane(t, k):
        return lax.ppermute(t, "dp", [(i, i ^ k) for i in range(ranks)])

    def ordered(parts, axis):
        odd, far = place % 2 == 1, place >= 2
        near = [jnp.where(odd, parts[1], parts[0]), jnp.where(odd, parts[0], parts[1])]
        rest = [jnp.where(odd, parts[3], parts[2]), jnp.where(odd, parts[2], parts[3])]
        out = [jnp.where(far, b, a) for a, b in zip(near, rest)]
        out += [jnp.where(far, a, b) for a, b in zip(near, rest)]
        return jnp.stack(out, axis)

    def exchange(parts):
        return [parts[0]] + [plane(parts[k], k) for k in range(1, PLANE)]

    def pick(t, axis):
        return [
            lax.dynamic_index_in_dim(t, place ^ k, axis, keepdims=False) for k in range(PLANE)
        ]

    def both(own, other, axis):
        return jnp.where(
            first,
            jnp.concatenate([own, other], axis),
            jnp.concatenate([other, own], axis),
        )

    def halves(t, axis):
        size = t.shape[axis] // 2
        own = lax.dynamic_slice_in_dim(t, core * size, size, axis)
        return own, lax.dynamic_slice_in_dim(t, (1 - core) * size, size, axis)

    shard = gain_mix.shape[0]
    gains = jnp.pad(jnp.stack([gain_mix, gain_feed], 1), ((0, 0), (0, 126)))
    pack_first = jnp.concatenate([w_value, w_out.T, gains], 1)
    pack_first = lax.all_gather(pack_first, "dp", axis=0, tiled=True)

    table_own, table_other = halves(mix_table, 2)
    table_other = sibling(table_other)
    table = both(table_own, table_other, 0)
    heads = table.shape[0] // PLANE
    local_rows = table.shape[1]
    half = seq // 2
    table = table.reshape(PLANE, heads, local_rows, half)
    table = ordered(exchange(pick(table, 0)), 1).reshape(heads, PLANE * local_rows, half)
    table = lax.all_gather(table, "dp", axis=0, axis_index_groups=lines)

    pack_feed = jnp.concatenate([w_up, w_down.T], 1)
    pack_feed = lax.all_gather(pack_feed, "dp", axis=0, tiled=True)
    table_mate = sibling(table)

    own_in, other_in = halves(inputs, 0)
    own_grad, other_grad = halves(out_grad, 0)
    lens, _ = halves(lengths, 0)
    live = lax.iota(jnp.int32, seq)[None, :] < lens[:, None]
    x = both(own_in, sibling(other_in), 2).astype(F32)
    grad_rows = jnp.where(live[:, :, None], both(own_grad, sibling(other_grad), 2), 0)
    group_lens = jnp.stack(exchange([lens] * PLANE)).reshape(-1)
    masks = (lax.iota(jnp.int32, seq)[None, :] < group_lens[:, None]).astype(BF16)
    masks = jnp.pad(masks, ((0, 8), (0, 0)))

    value_part = w_value.shape[1]
    first_other = sibling(pack_first)
    w_value = both(pack_first[:, :value_part], first_other[:, :value_part], 1)
    w_out_t = both(
        pack_first[:, value_part : 2 * value_part],
        first_other[:, value_part : 2 * value_part],
        1,
    )
    gain_mix = pack_first[:, 2 * value_part].astype(F32)
    gain_feed = pack_first[:, 2 * value_part + 1].astype(F32)

    scale_mix = lax.rsqrt(jnp.mean(x * x, axis=-1, keepdims=True) + EPSILON)
    normed = (x * scale_mix * gain_mix).astype(BF16)
    value = jnp.einsum("sti,ic->sct", normed, w_value, preferred_element_type=F32)
    value = jnp.where(live[:, None, :], value, 0.0).astype(BF16)
    value = value.reshape(mine, PLANE, heads, HEAD_DIM, seq)
    values = exchange(pick(value, 1))

    mixed_parts, inverse_sums, expo_table = mix_forward(core_ref, table, table_mate, values, masks)
    mixed = ordered(exchange(mixed_parts), 1).reshape(mine, features, seq)
    hidden = x + jnp.einsum("sct,oc->sto", mixed, w_out_t, preferred_element_type=F32)

    feed_other = sibling(pack_feed)
    width = w_up.shape[1]
    up = (pack_feed[:, :width], feed_other[:, :width])
    down = (pack_feed[:, width:], feed_other[:, width:])
    flat = lambda t: t.reshape(-1, t.shape[-1])
    output, grad_hidden, grad_low, act, grad_up, normed_feed, feed_gain_terms = feed(
        lens, flat(hidden), flat(grad_rows), gain_feed[None], up, down
    )
    grad_low = grad_low.reshape(mine, seq, features)

    grad_mixed = jnp.einsum("sto,oc->sct", grad_low, w_out_t, preferred_element_type=F32)
    grad_mixed = grad_mixed.astype(BF16).reshape(mine, PLANE, heads, HEAD_DIM, seq)
    grads = exchange(pick(grad_mixed, 1))
    keep, send, value_parts = mix_backward(
        core_ref, expo_table, values, grads, mixed_parts, inverse_sums, masks, blocks
    )

    table_grad = (keep.astype(F32) + sibling(send).astype(F32)).astype(BF16)
    table_grad = lax.psum_scatter(
        table_grad, "dp", scatter_dimension=0, axis_index_groups=lines, tiled=False
    )
    table_grad = table_grad.reshape(heads, PLANE, local_rows, half)
    table_grad = ordered(exchange(pick(table_grad, 1)), 0)
    table_grad = table_grad.reshape(PLANE * heads, local_rows, half)
    table_own, table_other = halves(table_grad, 0)
    table_grad = both(table_own, sibling(table_other), 2).astype(F32)

    up_grad = jnp.einsum("ti,tf->if", normed_feed, grad_up, preferred_element_type=F32)
    down_grad = jnp.einsum("ti,tf->if", flat(grad_rows), act, preferred_element_type=F32)
    own = jnp.concatenate([up_grad[:, :width], down_grad[:, :width]], 1)
    other = jnp.concatenate([up_grad[:, width:], down_grad[:, width:]], 1).astype(BF16)
    own = (own + sibling(other).astype(F32)).astype(BF16)
    own = lax.psum_scatter(own, "dp", scatter_dimension=0, tiled=True).astype(F32)
    up_grad, down_grad = own[:, :width], own[:, width:].T

    grad_value = ordered(exchange(value_parts), 1).reshape(mine, features, seq)
    value_grad = jnp.einsum("sti,sct->ic", normed, grad_value, preferred_element_type=F32)
    projection_grad = jnp.einsum("sto,sct->oc", grad_low, mixed, preferred_element_type=F32)
    grad_norm = jnp.einsum("sct,ic->sti", grad_value, w_value, preferred_element_type=F32)
    mix_gain_grad = jnp.sum(grad_norm * x * scale_mix, axis=(0, 1))
    feed_gain_grad = jnp.sum(feed_gain_terms, axis=0)
    scaled = grad_norm * gain_mix
    grad_in = (
        grad_hidden.reshape(x.shape)
        + scale_mix * scaled
        - x * (scale_mix * scale_mix * scale_mix) * jnp.mean(scaled * x, axis=-1, keepdims=True)
    )

    gain_grads = jnp.pad(jnp.stack([mix_gain_grad, feed_gain_grad], 1), ((0, 0), (0, 126)))
    gain_grads = gain_grads.astype(BF16)
    value_own, value_other = halves(value_grad, 1)
    projection_own, projection_other = halves(projection_grad, 1)
    other = jnp.concatenate(
        [value_other.astype(BF16), projection_other.astype(BF16), gain_grads], 1
    )
    own = jnp.concatenate([value_own, projection_own, gain_grads.astype(F32)], 1)
    own = (own + sibling(other).astype(F32)).astype(BF16)
    own = lax.psum_scatter(own, "dp", scatter_dimension=0, tiled=True).astype(F32)
    value_grad = own[:, :value_part]
    projection_grad = own[:, value_part : 2 * value_part].T
    mix_gain_grad = own[:, 2 * value_part]
    feed_gain_grad = own[:, 2 * value_part + 1]

    def placed(t):
        kept, sent = halves(t, 2)
        return both(kept, sibling(sent), 0)

    return (
        placed(output.reshape(mine, seq, features)),
        placed(grad_in.astype(BF16)),
        mix_gain_grad,
        value_grad,
        table_grad,
        projection_grad,
        feed_gain_grad,
        up_grad,
        down_grad,
    )


def solution(mesh):
    return jax.shard_map(
        body,
        mesh=mesh,
        in_specs=(
            P("dp", None, "head"),
            P("dp"),
            P("dp"),
            P("dp", "head"),
            P("head", "dp", None),
            P("head", "dp"),
            P("dp"),
            P("dp", "head"),
            P("head", "dp"),
            P("dp", None, "head"),
        ),
        out_specs=(
            P("dp", None, "head"),
            P("dp", None, "head"),
            P("dp"),
            P("dp", "head"),
            P("head", "dp", None),
            P("head", "dp"),
            P("dp"),
            P("dp", "head"),
            P("head", "dp"),
        ),
        check_vma=False,
    )
```

time: 2450 us -> 845 us (0.34)
  matrix products: 571 us -> 62 us
  waiting for transfers between devices: 960 us -> 528 us
  local copies, waits for them, and re-layouts: 387 us -> 61.6 us
  other arithmetic: 288 us -> 50.7 us
  blocking collectives: 180 us -> 0 us
  Pallas kernels: 0 us -> 87.3 us
  loops' own time: 33.3 us -> 0 us
  starting transfers between devices: 0.6 us -> 29.9 us
    reduce_scatter x5 -> x2, waiting for transfers between devices: 759 us -> 137 us  [the longest x1 137 us: body(): lax.psum_scatter(own, 'dp', scatter_dimension=0, tiled=True).astype(F32)]
    dot_general x48 -> x8, matrix products: 476 us -> 62 us  [the longest x1 16.7 us: body(): jnp.einsum('ti,tf->if', flat(grad_rows), act, preferred_element_type=F32)]
    dynamic_update_slice x16 -> x0, local copies, waits for them, and re-layouts: 284 us -> none  [the longest x8 275 us: block_back(): lax.dynamic_update_slice_in_dim(table_acc, earlier + grad_scores, row_sta...]
    sub x16 -> x0, other arithmetic: 187 us -> none  [table_probs(): return jax.nn.softmax(scores, axis=-1)]
    ppermute x0 -> x33, waiting for transfers between devices: none -> 137 us  [the longest x21 134 us: plane(): return lax.ppermute(t, 'dp', [(i, i ^ k) for i in range(ranks)])]
    sub x8 -> x0, matrix products: 94.6 us -> none  [block_back(): grad_probs - jnp.sum(grad_probs * prob_block, axis=-1, keepdims=True)]
    all_gather x2 -> x0, blocking collectives: 93.2 us -> none  [the longest x1 49.8 us: body(): lax.all_gather(w_out, 'dp', axis=1, tiled=True)]
    pallas_call x0 -> x3, Pallas kernels: none -> 87.3 us  [the longest x1 54.3 us: feed(): pl.pallas_call(feed_kernel, grid_spec=pltpu.PrefetchScalarGridSpec(num_sc...]
  transfers between devices with their start and end apart: 15 -> 39, of which waited for: 9 -> 21; matrix products, arithmetic and copies ran while one was open for 41% -> 17% of each run, Pallas kernels for 0% -> 2%
where the time goes in v1:
time: 845 us; the launch traced here: 835 us
  waiting for transfers between devices  528 us (62%)
  Pallas kernels  87.3 us (10%)
  matrix products  62 us (7%)
  local copies, waits for them, and re-layouts  61.6 us (7%)
  other arithmetic  50.7 us (6%)
  starting transfers between devices  29.9 us (4%)
  between operations  14.9 us (2%)
    reduce_scatter x1, waiting for transfers between devices, body(): lax.psum_scatter(own, 'dp', scatter_dimension=0, tiled=True).astype(F32)  137 us
    ppermute x21, waiting for transfers between devices, plane(): return lax.ppermute(t, 'dp', [(i, i ^ k) for i in range(ranks)])  134 us
    unnamed x7, waiting for transfers between devices  81.4 us
    all_gather x1, waiting for transfers between devices, body(): pack_feed = lax.all_gather(pack_feed, 'dp', axis=0, tiled=True)  73.1 us
    all_gather x1, waiting for transfers between devices, body(): table = lax.all_gather(table, 'dp', axis=0, axis_index_groups=lines)  61 us
    pallas_call x1, Pallas kernels, feed(): pl.pallas_call(feed_kernel, grid_spec=pltpu.PrefetchScalarGridSpec(num_sc...  54.3 us
    all_gather x1, waiting for transfers between devices, body(): pack_first = lax.all_gather(pack_first, 'dp', axis=0, tiled=True)  38.9 us
    ppermute x21, starting transfers between devices, plane(): return lax.ppermute(t, 'dp', [(i, i ^ k) for i in range(ranks)])  27.4 us
  transfers between devices with their start and end apart: 39, of which 21 were waited for; matrix products, arithmetic and copies ran while one was open for 17% of the time, Pallas kernels for 2%

profile of v1, /device:TPU:0, one launch (start us, length us, event | category | flops | bytes accessed | tf_op | source)
XLA Modules:
  0.0 834.6 jit_solution(5667981881237521140)
XLA Ops:
  12.8 3.9 collective-permute-start.2
  17.3 5.1 collective-permute-done.2
  22.4 4.3 collective-permute-done.3
  32.3 38.9 %all-gather.6.cloned.1.call-done = bf16[768,896]{1,0:T(8,128)(2,1)} async-done(((bf16[48,896]{1,0:T(8,128)(2,1)}), bf16[768,896]{1,0:T(8,128)(2,1)}) %all-gather.6.cloned.1.call-update) | async-done | bytes 1376272 | tf_op jit(solution)/shard_map/all_gather | solution.py:321
  74.5 61.0 %all-gather.4.cloned.1.call-done.ta = bf16[4,3,256,512]{3,2,1,0:T(8,128)(2,1)} async-done(((bf16[1,3,256,512]{3,2,1,0:T(8,128)(2,1)}), bf16[4,3,256,512]{3,2,1,0:T(8,128)(2,1)}) %all-gather.4.cloned.1.call-update) | async-done | bytes 3145744 | tf_op jit(solution)/shard_map/all_gather | solution.py:331
  146.4 73.1 %all-gather.8.cloned.1.call-done = bf16[768,3072]{1,0:T(8,128)(2,1)} async-done(((bf16[48,3072]{1,0:T(8,128)(2,1)}), bf16[768,3072]{1,0:T(8,128)(2,1)}) %all-gather.8.cloned.1.call-update) | async-done | bytes 4718608 | tf_op jit(solution)/shard_map/all_gather | solution.py:334
  239.2 29.4 %collective-permute-done.8.v2 = bf16[2,3,64,1024]{3,2,1,0:T(8,128)(2,1)} collective-permute-done((bf16[2,3,64,1024]{3,2,1,0:T(8,128)(2,1)}, bf16[2,3,64,1024]{3,2,1,0:T(8,128)(2,1)}, u32[]{:S(2)}, u32[]{:S(2)}) %collective-permute-start.8) | collective-permute-done | bytes 786464 | tf_op jit(solution)/shard_map/ppermute | solution.py:288
  268.6 14.6 %shard_map.169 = (bf16[2,3,64,1024]{3,2,1,0:T(8,128)(2,1)}, bf16[2,3,64,1024]{3,2,1,0:T(8,128)(2,1)}, bf16[2,3,64,1024]{3,2,1,0:T(8,128)(2,1)}, bf16[2,3,64,1024...) custom-call(s32[1]{0:T(128)} %bitcast.core, ...), custom_call_target="tpu_custom_call" | custom-call | flops 3271557120 | bytes 12582912 | tf_op jit(solution)/shard_map/pallas_call | solution.py:122
  286.8 4.0 fusion.10.grad
  293.7 11.1 %collective-permute-done.13 = bf16[2,3,64,1024]{3,2,1,0:T(8,128)(2,1)S(1)} collective-permute-done((bf16[2,3,64,1024]{3,2,1,0:T(8,128)(2,1)}, bf16[2,3,64,1024]{3,2,1,0:T(8,128)(2,1)S(1)}, u32[]{:S(2)}, u32[]{:S(2)}) %collective-permute-start.13) | collective-permute-done | bytes 786464 | tf_op jit(solution)/shard_map/ppermute | solution.py:288
  304.9 13.7 %collective-permute-done.14 = bf16[2,3,64,1024]{3,2,1,0:T(8,128)(2,1)S(1)} collective-permute-done((bf16[2,3,64,1024]{3,2,1,0:T(8,128)(2,1)}, bf16[2,3,64,1024]{3,2,1,0:T(8,128)(2,1)S(1)}, u32[]{:S(2)}, u32[]{:S(2)}) %collective-permute-start.14) | collective-permute-done | bytes 786464 | tf_op jit(solution)/shard_map/ppermute | solution.py:288
  321.5 7.2 convert_add_fusion
  328.7 4.9 fusion.39
  333.6 54.3 %shard_map.170 = (bf16[2048,768]{1,0:T(8,128)(2,1)}, f32[2048,768]{1,0:T(8,128)}, bf16[2048,768]{1,0:T(8,128)(2,1)}, bf16[2048,3072]{1,0:T(8,128)(2,1)}, bf16[20...) custom-call(s32[2]{0:T(128)} %copy-done.22, f32[2048,768]{1,0:T(8,128)} %bitcast.189, ...), custom_call_target="tpu_custom_call" | custom-call | flops 38654705664 | bytes 59768832 | tf_op jit(solution)/shard_map/pallas_call | solution.py:236
  387.9 5.4 convolution_convert_fusion
  398.1 17.0 %collective-permute-done.19.g1 = bf16[2,3,64,1024]{3,2,1,0:T(8,128)(2,1)S(1)} collective-permute-done((bf16[2,3,64,1024]{3,2,1,0:T(8,128)(2,1)S(1)}, bf16[2,3,64,1024]{3,2,1,0:T(8,128)(2,1)S(1)}, u32[]{:S(2)}, u32[]{:S(2)}) %collective-permute-start.19) | collective-permute-done | bytes 786464 | tf_op jit(solution)/shard_map/ppermute | solution.py:288
  415.0 16.9 %collective-permute-done.20.g2 = bf16[2,3,64,1024]{3,2,1,0:T(8,128)(2,1)S(1)} collective-permute-done((bf16[2,3,64,1024]{3,2,1,0:T(8,128)(2,1)S(1)}, bf16[2,3,64,1024]{3,2,1,0:T(8,128)(2,1)S(1)}, u32[]{:S(2)}, u32[]{:S(2)}) %collective-permute-start.20) | collective-permute-done | bytes 786464 | tf_op jit(solution)/shard_map/ppermute | solution.py:288
  433.2 18.5 %shard_map.171 = (bf16[4,3,256,512]{3,2,1,0:T(8,128)(2,1)}, bf16[4,3,256,512]{3,2,1,0:T(8,128)(2,1)}, bf16[2,3,64,1024]{3,2,1,0:T(8,128)(2,1)}, bf16[2,3,64,1024...) custom-call(s32[1]{0:T(128)} %bitcast.core, ...), custom_call_target="tpu_custom_call" | custom-call | flops 6543114240 | bytes 12582912 | tf_op jit(solution)/shard_map/pallas_call | solution.py:152
  451.7 16.7 %fusion.44 = f32[768,3072]{1,0:T(8,128)} fusion(bf16[2048,768]{1,0:T(8,128)(2,1)} %fusion.10.grad, bf16[2048,3072]{1,0:T(8,128)(2,1)} %get-tuple-element.46), kind=kOutput, calls=%fused_computation.141 | convolution fusion | flops 9663676416 | bytes 25165824 | tf_op jit(solution)/shard_map/ti,tf->if/dot_general | solution.py:397
  468.4 4.6 add_convert_fusion
  473.1 13.9 %fusion.43 = f32[768,3072]{1,0:T(8,128)S(1)} fusion(bf16[2048,768]{1,0:T(8,128)(2,1)} %get-tuple-element.44, bf16[2048,3072]{1,0:T(8,128)(2,1)} %get-tuple-element.45), kind=kOutput, calls=%fused_computation.140 | convolution fusion | flops 9663676416 | bytes 25165824 | tf_op jit(solution)/shard_map/ti,tf->if/dot_general | solution.py:396
  500.4 5.4 convolution_bitcast_fusion
  505.9 12.5 %collective-permute-done.22 = bf16[2,3,64,1024]{3,2,1,0:T(8,128)(2,1)S(1)} collective-permute-done((bf16[2,3,64,1024]{3,2,1,0:T(8,128)(2,1)}, bf16[2,3,64,1024]{3,2,1,0:T(8,128)(2,1)S(1)}, u32[]{:S(2)}, u32[]{:S(2)}) %collective-permute-start.22) | collective-permute-done | bytes 786464 | tf_op jit(solution)/shard_map/ppermute | solution.py:288
  518.5 15.9 %collective-permute-done.23 = bf16[2,3,64,1024]{3,2,1,0:T(8,128)(2,1)S(1)} collective-permute-done((bf16[2,3,64,1024]{3,2,1,0:T(8,128)(2,1)}, bf16[2,3,64,1024]{3,2,1,0:T(8,128)(2,1)S(1)}, u32[]{:S(2)}, u32[]{:S(2)}) %collective-permute-start.23) | collective-permute-done | bytes 786464 | tf_op jit(solution)/shard_map/ppermute | solution.py:288
  536.5 7.3 fusion.9
  557.5 4.8 slice.96
  562.3 4.9 slice.97
  567.2 9.0 %fusion = bf16[768,3072]{1,0:T(8,128)(2,1)} fusion(f32[768,1536]{1,0:T(8,128)} %slice.97, f32[768,1536]{1,0:T(8,128)} %slice.96, bf16[768,3072]{1,0:T(8,128)(2,1)} %collective-permute-done.32), kind=kLoop, calls=%fused_computation.7 | loop fusion | flops 9437184 | bytes 18874368 | tf_op jit(solution)/shard_map/convert_element_type | solution.py:400
  576.2 3.9 constant_dynamic-slice_fusion.7
  580.3 6.4 fusion.6
  600.2 81.3 %reduce-scatter.10.cloned.1.call-done = bf16[48,896]{1,0:T(8,128)(2,1)} async-done(((bf16[768,896]{1,0:T(8,128)(2,1)}), bf16[48,896]{1,0:T(8,128)(2,1)}) %reduce-scatter.10.cloned.1.call-update) | async-done | bytes 86032
  687.3 136.9 %reduce-scatter.8.cloned.1.call-done = bf16[48,3072]{1,0:T(8,128)(2,1)} async-done(((bf16[768,3072]{1,0:T(8,128)(2,1)}), bf16[48,3072]{1,0:T(8,128)(2,1)}) %reduce-scatter.8.cloned.1.call-update) | async-done | bytes 294928 | tf_op jit(solution)/shard_map/reduce_scatter | solution.py:401
  (192 shorter events, 113.0 us)
Async XLA Ops:
  7.2 64.0 %all-gather.6.cloned.1.call-start = ((), (), s32[]{:S(2)}) async-start(), calls=%async_computation.4 | async-start | bytes 1462272 | tf_op jit(solution)/shard_map/all_gather | solution.py:321
  9.5 126.0 %all-gather.4.cloned.1.call-start = ((), (), s32[]{:S(2)}) async-start(), calls=%async_computation.3 | async-start | bytes 3932160 | tf_op jit(solution)/shard_map/all_gather | solution.py:331
  12.8 9.6 %collective-permute-start.2 = (bf16[3,64,512]{2,1,0:T(8,128)(2,1)S(1)}, bf16[3,64,512]{2,1,0:T(8,128)(2,1)S(1)}, u32[]{:S(2)}, u32[]{:S(2)}) collective-permute-start(bf16[3,64,512]{2,1,0:T(8,128)(2,1)S(1)} %get-tuple-element.125), channel_id=1, source_target_pairs={{0,6},{2,4},{4,2},{6,0},{8,14},{10,12},{12,10},{14,8},{16,22},{18,... | collective-permute-start | bytes 589832 | tf_op jit(solution)/shard_map/ppermute | solution.py:288
  16.6 10.0 %collective-permute-start.3 = (bf16[3,64,512]{2,1,0:T(8,128)(2,1)S(1)}, bf16[3,64,512]{2,1,0:T(8,128)(2,1)S(1)}, u32[]{:S(2)}, u32[]{:S(2)}) collective-permute-start(bf16[3,64,512]{2,1,0:T(8,128)(2,1)S(1)} %get-tuple-element.124), channel_id=1, source_target_pairs={{0,4},{2,6},{4,0},{6,2},{8,12},{10,14},{12,8},{14,10},{16,20},{18,... | collective-permute-start | bytes 589832 | tf_op jit(solution)/shard_map/ppermute | solution.py:288
  17.1 9.8 %collective-permute-start.4 = (bf16[3,64,512]{2,1,0:T(8,128)(2,1)S(1)}, bf16[3,64,512]{2,1,0:T(8,128)(2,1)S(1)}, u32[]{:S(2)}, u32[]{:S(2)}) collective-permute-start(bf16[3,64,512]{2,1,0:T(8,128)(2,1)S(1)} %get-tuple-element.123), channel_id=1, source_target_pairs={{0,2},{2,0},{4,6},{6,4},{8,10},{10,8},{12,14},{14,12},{16,18},{18,... | collective-permute-start | bytes 589832 | tf_op jit(solution)/shard_map/ppermute | solution.py:288
  28.0 191.5 %all-gather.8.cloned.1.call-start = ((), (), s32[]{:S(2)}) async-start(), calls=%async_computation.5 | async-start | bytes 5013504 | tf_op jit(solution)/shard_map/all_gather | solution.py:334
  28.9 563.2 %reduce-scatter.6.cloned.1.call-start = ((), (), s32[]{:S(2)}) async-start(), calls=%async_computation.6 | async-start | bytes 3932160 | tf_op jit(solution)/shard_map/reduce_scatter | solution.py:387
  32.3 39.1 %collective-permute-start = (bf16[2,1024,384]{2,1,0:T(8,128)(2,1)}, bf16[2,1024,384]{2,1,0:T(8,128)(2,1)S(1)}, u32[]{:S(2)}, u32[]{:S(2)}) collective-permute-start(bf16[2,1024,384]{2,1,0:T(8,128)(2,1)} %get-tuple-element.104), channel_id=1, source_target_pairs={{0,1},{1,0},{2,3},{3,2},{4,5},{5,4},{6,7},{7,6},{8,9},{9,8},{10,11... | collective-permute-start | bytes 4718600 | tf_op jit(solution)/shard_map/ppermute | solution.py:285
  71.2 66.5 %collective-permute-start.6 = (bf16[768,896]{1,0:T(8,128)(2,1)}, bf16[768,896]{1,0:T(8,128)(2,1)}, u32[]{:S(2)}, u32[]{:S(2)}) collective-permute-start(bf16[768,896]{1,0:T(8,128)(2,1)} %all-gather.6.cloned.1.call-done), channel_id=1, source_target_pairs={{0,1},{1,0},{2,3},{3,2},{4,5},{5,4},{6,7},{7,6},{8,9},{9,8},{10,11... | collective-permute-start | bytes 4128776 | tf_op jit(solution)/shard_map/ppermute | solution.py:285
  135.5 133.1 %collective-permute-start.5 = (bf16[4,3,256,512]{3,2,1,0:T(8,128)(2,1)}, bf16[4,3,256,512]{3,2,1,0:T(8,128)(2,1)}, u32[]{:S(2)}, u32[]{:S(2)}) collective-permute-start(bf16[4,3,256,512]{3,2,1,0:T(8,128)(2,1)} %all-gather.4.cloned.1.call-done.ta), channel_id=1, source_target_pairs={{0,1},{1,0},{2,3},{3,2},{4,5},{5,4},{6,7},{7,6},{8,9},{9,8},{10,11... | collective-permute-start | bytes 9437192 | tf_op jit(solution)/shard_map/ppermute | solution.py:285
  145.0 91.9 %collective-permute-start.7 = (bf16[2,3,64,1024]{3,2,1,0:T(8,128)(2,1)}, bf16[2,3,64,1024]{3,2,1,0:T(8,128)(2,1)}, u32[]{:S(2)}, u32[]{:S(2)}) collective-permute-start(bf16[2,3,64,1024]{3,2,1,0:T(8,128)(2,1)} %get-tuple-element.102), channel_id=1, source_target_pairs={{0,2},{2,0},{4,6},{6,4},{8,10},{10,8},{12,14},{14,12},{16,18},{18,... | collective-permute-start | bytes 2359304 | tf_op jit(solution)/shard_map/ppermute | solution.py:288
  219.5 109.2 %collective-permute-start.17 = (bf16[768,3072]{1,0:T(8,128)(2,1)}, bf16[768,3072]{1,0:T(8,128)(2,1)}, u32[]{:S(2)}, u32[]{:S(2)}) collective-permute-start(bf16[768,3072]{1,0:T(8,128)(2,1)} %all-gather.8.cloned.1.call-done), channel_id=1, source_target_pairs={{0,1},{1,0},{2,3},{3,2},{4,5},{5,4},{6,7},{7,6},{8,9},{9,8},{10,11... | collective-permute-start | bytes 14155784 | tf_op jit(solution)/shard_map/ppermute | solution.py:285
  223.4 63.4 %collective-permute-start.16 = (bf16[2,1024,384]{2,1,0:T(8,128)(2,1)}, bf16[2,1024,384]{2,1,0:T(8,128)(2,1)}, u32[]{:S(2)}, u32[]{:S(2)}) collective-permute-start(bf16[2,1024,384]{2,1,0:T(8,128)(2,1)} %get-tuple-element.95), channel_id=1, source_target_pairs={{0,1},{1,0},{2,3},{3,2},{4,5},{5,4},{6,7},{7,6},{8,9},{9,8},{10,11... | collective-permute-start | bytes 4718600 | tf_op jit(solution)/shard_map/ppermute | solution.py:285
  235.4 33.2 %collective-permute-start.8 = (bf16[2,3,64,1024]{3,2,1,0:T(8,128)(2,1)}, bf16[2,3,64,1024]{3,2,1,0:T(8,128)(2,1)}, u32[]{:S(2)}, u32[]{:S(2)}) collective-permute-start(bf16[2,3,64,1024]{3,2,1,0:T(8,128)(2,1)} %get-tuple-element.101), channel_id=1, source_target_pairs={{0,4},{2,6},{4,0},{6,2},{8,12},{10,14},{12,8},{14,10},{16,20},{18,... | collective-permute-start | bytes 2359304 | tf_op jit(solution)/shard_map/ppermute | solution.py:288
  236.9 31.7 %collective-permute-start.9 = (bf16[2,3,64,1024]{3,2,1,0:T(8,128)(2,1)}, bf16[2,3,64,1024]{3,2,1,0:T(8,128)(2,1)}, u32[]{:S(2)}, u32[]{:S(2)}) collective-permute-start(bf16[2,3,64,1024]{3,2,1,0:T(8,128)(2,1)} %get-tuple-element.100), channel_id=1, source_target_pairs={{0,6},{2,4},{4,2},{6,0},{8,14},{10,12},{12,10},{14,8},{16,22},{18,... | collective-permute-start | bytes 2359304 | tf_op jit(solution)/shard_map/ppermute | solution.py:288
  283.2 21.7 %collective-permute-start.13 = (bf16[2,3,64,1024]{3,2,1,0:T(8,128)(2,1)}, bf16[2,3,64,1024]{3,2,1,0:T(8,128)(2,1)S(1)}, u32[]{:S(2)}, u32[]{:S(2)}) collective-permute-start(bf16[2,3,64,1024]{3,2,1,0:T(8,128)(2,1)} %get-tuple-element.28.x3), channel_id=1, source_target_pairs={{0,6},{2,4},{4,2},{6,0},{8,14},{10,12},{12,10},{14,8},{16,22},{18,... | collective-permute-start | bytes 2359304 | tf_op jit(solution)/shard_map/ppermute | solution.py:288
  284.7 33.8 %collective-permute-start.14 = (bf16[2,3,64,1024]{3,2,1,0:T(8,128)(2,1)}, bf16[2,3,64,1024]{3,2,1,0:T(8,128)(2,1)S(1)}, u32[]{:S(2)}, u32[]{:S(2)}) collective-permute-start(bf16[2,3,64,1024]{3,2,1,0:T(8,128)(2,1)} %get-tuple-element.29.x2), channel_id=1, source_target_pairs={{0,4},{2,6},{4,0},{6,2},{8,12},{10,14},{12,8},{14,10},{16,20},{18,... | collective-permute-start | bytes 2359304 | tf_op jit(solution)/shard_map/ppermute | solution.py:288
  286.2 33.3 %collective-permute-start.15 = (bf16[2,3,64,1024]{3,2,1,0:T(8,128)(2,1)}, bf16[2,3,64,1024]{3,2,1,0:T(8,128)(2,1)S(1)}, u32[]{:S(2)}, u32[]{:S(2)}) collective-permute-start(bf16[2,3,64,1024]{3,2,1,0:T(8,128)(2,1)} %get-tuple-element.30.x1), channel_id=1, source_target_pairs={{0,2},{2,0},{4,6},{6,4},{8,10},{10,8},{12,14},{14,12},{16,18},{18,... | collective-permute-start | bytes 2359304 | tf_op jit(solution)/shard_map/ppermute | solution.py:288
  394.6 20.5 %collective-permute-start.19 = (bf16[2,3,64,1024]{3,2,1,0:T(8,128)(2,1)S(1)}, bf16[2,3,64,1024]{3,2,1,0:T(8,128)(2,1)S(1)}, u32[]{:S(2)}, u32[]{:S(2)}) collective-permute-start(bf16[2,3,64,1024]{3,2,1,0:T(8,128)(2,1)S(1)} %get-tuple-element.90), channel_id=1, source_target_pairs={{0,2},{2,0},{4,6},{6,4},{8,10},{10,8},{12,14},{14,12},{16,18},{18,... | collective-permute-start | bytes 2359304 | tf_op jit(solution)/shard_map/ppermute | solution.py:288
  395.9 36.0 %collective-permute-start.20 = (bf16[2,3,64,1024]{3,2,1,0:T(8,128)(2,1)S(1)}, bf16[2,3,64,1024]{3,2,1,0:T(8,128)(2,1)S(1)}, u32[]{:S(2)}, u32[]{:S(2)}) collective-permute-start(bf16[2,3,64,1024]{3,2,1,0:T(8,128)(2,1)S(1)} %get-tuple-element.89), channel_id=1, source_target_pairs={{0,4},{2,6},{4,0},{6,2},{8,12},{10,14},{12,8},{14,10},{16,20},{18,... | collective-permute-start | bytes 2359304 | tf_op jit(solution)/shard_map/ppermute | solution.py:288
  396.6 35.4 %collective-permute-start.21 = (bf16[2,3,64,1024]{3,2,1,0:T(8,128)(2,1)S(1)}, bf16[2,3,64,1024]{3,2,1,0:T(8,128)(2,1)S(1)}, u32[]{:S(2)}, u32[]{:S(2)}) collective-permute-start(bf16[2,3,64,1024]{3,2,1,0:T(8,128)(2,1)S(1)} %get-tuple-element.88), channel_id=1, source_target_pairs={{0,6},{2,4},{4,2},{6,0},{8,14},{10,12},{12,10},{14,8},{16,22},{18,... | collective-permute-start | bytes 2359304 | tf_op jit(solution)/shard_map/ppermute | solution.py:288
  451.6 16.8 %collective-permute-start.27 = (bf16[4,3,256,512]{3,2,1,0:T(8,128)(2,1)}, bf16[4,3,256,512]{3,2,1,0:T(8,128)(2,1)}, u32[]{:S(2)}, u32[]{:S(2)}) collective-permute-start(bf16[4,3,256,512]{3,2,1,0:T(8,128)(2,1)} %get-tuple-element.43), channel_id=1, source_target_pairs={{0,1},{1,0},{2,3},{3,2},{4,5},{5,4},{6,7},{7,6},{8,9},{9,8},{10,11... | collective-permute-start | bytes 9437192 | tf_op jit(solution)/shard_map/ppermute | solution.py:285
  473.0 208.4 %reduce-scatter.10.cloned.1.call-start = ((), (), s32[]{:S(2)}) async-start(), calls=%async_computation.8 | async-start | bytes 1462272
  496.4 70.8 %collective-permute-start.32 = (bf16[768,3072]{1,0:T(8,128)(2,1)}, bf16[768,3072]{1,0:T(8,128)(2,1)}, u32[]{:S(2)}, u32[]{:S(2)}) collective-permute-start(bf16[768,3072]{1,0:T(8,128)(2,1)} %pad_maximum_fusion), channel_id=1, source_target_pairs={{0,1},{1,0},{2,3},{3,2},{4,5},{5,4},{6,7},{7,6},{8,9},{9,8},{10,11... | collective-permute-start | bytes 14155784 | tf_op jit(solution)/shard_map/ppermute | solution.py:285
  496.8 21.6 %collective-permute-start.22 = (bf16[2,3,64,1024]{3,2,1,0:T(8,128)(2,1)}, bf16[2,3,64,1024]{3,2,1,0:T(8,128)(2,1)S(1)}, u32[]{:S(2)}, u32[]{:S(2)}) collective-permute-start(bf16[2,3,64,1024]{3,2,1,0:T(8,128)(2,1)} %get-tuple-element.37), channel_id=1, source_target_pairs={{0,6},{2,4},{4,2},{6,0},{8,14},{10,12},{12,10},{14,8},{16,22},{18,... | collective-permute-start | bytes 2359304 | tf_op jit(solution)/shard_map/ppermute | solution.py:288
  498.4 36.0 %collective-permute-start.23 = (bf16[2,3,64,1024]{3,2,1,0:T(8,128)(2,1)}, bf16[2,3,64,1024]{3,2,1,0:T(8,128)(2,1)S(1)}, u32[]{:S(2)}, u32[]{:S(2)}) collective-permute-start(bf16[2,3,64,1024]{3,2,1,0:T(8,128)(2,1)} %get-tuple-element.38), channel_id=1, source_target_pairs={{0,4},{2,6},{4,0},{6,2},{8,12},{10,14},{12,8},{14,10},{16,20},{18,... | collective-permute-start | bytes 2359304 | tf_op jit(solution)/shard_map/ppermute | solution.py:288
  498.7 35.7 %collective-permute-start.24 = (bf16[2,3,64,1024]{3,2,1,0:T(8,128)(2,1)}, bf16[2,3,64,1024]{3,2,1,0:T(8,128)(2,1)S(1)}, u32[]{:S(2)}, u32[]{:S(2)}) collective-permute-start(bf16[2,3,64,1024]{3,2,1,0:T(8,128)(2,1)} %get-tuple-element.39), channel_id=1, source_target_pairs={{0,2},{2,0},{4,6},{6,4},{8,10},{10,8},{12,14},{14,12},{16,18},{18,... | collective-permute-start | bytes 2359304 | tf_op jit(solution)/shard_map/ppermute | solution.py:288
  557.5 266.7 %reduce-scatter.8.cloned.1.call-start = ((), (), s32[]{:S(2)}) async-start(), calls=%async_computation.7 | async-start | bytes 5013504 | tf_op jit(solution)/shard_map/reduce_scatter | solution.py:401
  588.2 8.6 %collective-permute-start.25 = (bf16[2,1024,384]{2,1,0:T(8,128)(2,1)}, bf16[2,1024,384]{2,1,0:T(8,128)(2,1)}, u32[]{:S(2)}, u32[]{:S(2)}) collective-permute-start(bf16[2,1024,384]{2,1,0:T(8,128)(2,1)} %get-tuple-element.83), channel_id=1, source_target_pairs={{0,1},{1,0},{2,3},{3,2},{4,5},{5,4},{6,7},{7,6},{8,9},{9,8},{10,11... | collective-permute-start | bytes 4718600 | tf_op jit(solution)/shard_map/ppermute | solution.py:285
  593.3 89.3 %collective-permute-start.28 = (bf16[3,64,512]{2,1,0:T(8,128)(2,1)S(1)}, bf16[3,64,512]{2,1,0:T(8,128)(2,1)S(1)}, u32[]{:S(2)}, u32[]{:S(2)}) collective-permute-start(bf16[3,64,512]{2,1,0:T(8,128)(2,1)S(1)} %get-tuple-element.122), channel_id=1, source_target_pairs={{0,6},{2,4},{4,2},{6,0},{8,14},{10,12},{12,10},{14,8},{16,22},{18,... | collective-permute-start | bytes 589832 | tf_op jit(solution)/shard_map/ppermute | solution.py:288
  594.8 87.8 %collective-permute-start.29 = (bf16[3,64,512]{2,1,0:T(8,128)(2,1)S(1)}, bf16[3,64,512]{2,1,0:T(8,128)(2,1)S(1)}, u32[]{:S(2)}, u32[]{:S(2)}) collective-permute-start(bf16[3,64,512]{2,1,0:T(8,128)(2,1)S(1)} %get-tuple-element.121), channel_id=1, source_target_pairs={{0,4},{2,6},{4,0},{6,2},{8,12},{10,14},{12,8},{14,10},{16,20},{18,... | collective-permute-start | bytes 589832 | tf_op jit(solution)/shard_map/ppermute | solution.py:288
  595.4 87.2 %collective-permute-start.30 = (bf16[3,64,512]{2,1,0:T(8,128)(2,1)S(1)}, bf16[3,64,512]{2,1,0:T(8,128)(2,1)S(1)}, u32[]{:S(2)}, u32[]{:S(2)}) collective-permute-start(bf16[3,64,512]{2,1,0:T(8,128)(2,1)S(1)} %get-tuple-element.120), channel_id=1, source_target_pairs={{0,2},{2,0},{4,6},{6,4},{8,10},{10,8},{12,14},{14,12},{16,18},{18,... | collective-permute-start | bytes 589832 | tf_op jit(solution)/shard_map/ppermute | solution.py:288
  (34 other events, 453.9 us)
Sparse Core Ops, SparseCore 0:
  11.4 59.7 all-gather.5
  73.3 62.1 all-gather.3
  138.9 80.6 all-gather.7
  473.1 59.0 reduce-scatter.5
  557.6 123.8 reduce-scatter.9
  687.3 136.8 reduce-scatter.7

commit v2 on v1

--- a/solution.py
+++ b/solution.py
@@ -279,12 +279,13 @@
     features = 2 * feature_part
     first = core == 0
     core_ref = core.astype(jnp.int32).reshape(1)
+    cube_bits = [1 << b for b in range(ranks.bit_length() - 2, -1, -1)]
     lines = [[b * PLANE + q for b in range(blocks)] for q in range(PLANE)]
 
     def sibling(t):
         return lax.ppermute(t, "head", [(0, 1), (1, 0)])
 
-    def plane(t, k):
+    def chip(t, k):
         return lax.ppermute(t, "dp", [(i, i ^ k) for i in range(ranks)])
 
     def ordered(parts, axis):
@@ -296,7 +297,7 @@
         return jnp.stack(out, axis)
 
     def exchange(parts):
-        return [parts[0]] + [plane(parts[k], k) for k in range(1, PLANE)]
+        return [parts[0]] + [chip(parts[k], k) for k in range(1, PLANE)]
 
     def pick(t, axis):
         return [
@@ -315,10 +316,31 @@
         own = lax.dynamic_slice_in_dim(t, core * size, size, axis)
         return own, lax.dynamic_slice_in_dim(t, (1 - core) * size, size, axis)
 
-    shard = gain_mix.shape[0]
+    def cube_gather(t):
+        rows = t.shape[0]
+        axis = 0
+        for bit in cube_bits:
+            got = chip(t, bit)
+            upper = (rank & bit) != 0
+            t = jnp.where(upper, jnp.stack([got, t], axis), jnp.stack([t, got], axis))
+            axis += 1
+        return t.reshape(ranks * rows, -1)
+
+    def cube_fold(t, axis, bit):
+        upper = ((rank & bit) != 0).astype(jnp.int32)
+        sent = lax.dynamic_index_in_dim(t, 1 - upper, axis, keepdims=False)
+        kept = lax.dynamic_index_in_dim(t, upper, axis, keepdims=False)
+        return kept.astype(F32) + chip(sent.astype(BF16), bit).astype(F32)
+
+    def cube_scatter(t):
+        t = t.reshape((2,) * len(cube_bits) + (t.shape[0] // ranks, t.shape[1]))
+        for axis in range(len(cube_bits) - 1, -1, -1):
+            t = cube_fold(t, axis, cube_bits[axis])
+        return t
+
     gains = jnp.pad(jnp.stack([gain_mix, gain_feed], 1), ((0, 0), (0, 126)))
     pack_first = jnp.concatenate([w_value, w_out.T, gains], 1)
-    pack_first = lax.all_gather(pack_first, "dp", axis=0, tiled=True)
+    pack_first = cube_gather(pack_first)
 
     table_own, table_other = halves(mix_table, 2)
     table_other = sibling(table_other)
@@ -331,6 +353,7 @@
     table = lax.all_gather(table, "dp", axis=0, axis_index_groups=lines)
 
     pack_feed = jnp.concatenate([w_up, w_down.T], 1)
+    pack_feed, table = lax.optimization_barrier((pack_feed, table))
     pack_feed = lax.all_gather(pack_feed, "dp", axis=0, tiled=True)
     table_mate = sibling(table)
 
@@ -395,11 +418,17 @@
 
     up_grad = jnp.einsum("ti,tf->if", normed_feed, grad_up, preferred_element_type=F32)
     down_grad = jnp.einsum("ti,tf->if", flat(grad_rows), act, preferred_element_type=F32)
-    own = jnp.concatenate([up_grad[:, :width], down_grad[:, :width]], 1)
-    other = jnp.concatenate([up_grad[:, width:], down_grad[:, width:]], 1).astype(BF16)
-    own = (own + sibling(other).astype(F32)).astype(BF16)
-    own = lax.psum_scatter(own, "dp", scatter_dimension=0, tiled=True).astype(F32)
-    up_grad, down_grad = own[:, :width], own[:, width:].T
+    parts = []
+    for grad, order in ((up_grad, ((2, 1), (1, 2))), (down_grad, ((1, 2), (1, 1)))):
+        part = grad[:, :width] + sibling(grad[:, width:].astype(BF16)).astype(F32)
+        part = part.reshape(blocks, 2, 2, -1, width)
+        for axis, bit in order:
+            part = cube_fold(part, axis, bit)
+        parts.append(part.astype(BF16))
+    parts = lax.psum_scatter(
+        jnp.concatenate(parts, 2), "dp", scatter_dimension=0, axis_index_groups=lines, tiled=False
+    ).astype(F32)
+    up_grad, down_grad = parts[:, :width], parts[:, width:].T
 
     grad_value = ordered(exchange(value_parts), 1).reshape(mine, features, seq)
     value_grad = jnp.einsum("sti,sct->ic", normed, grad_value, preferred_element_type=F32)
@@ -422,8 +451,7 @@
         [value_other.astype(BF16), projection_other.astype(BF16), gain_grads], 1
     )
     own = jnp.concatenate([value_own, projection_own, gain_grads.astype(F32)], 1)
-    own = (own + sibling(other).astype(F32)).astype(BF16)
-    own = lax.psum_scatter(own, "dp", scatter_dimension=0, tiled=True).astype(F32)
+    own = cube_scatter(own + sibling(other).astype(F32))
     value_grad = own[:, :value_part]
     projection_grad = own[:, value_part : 2 * value_part].T
     mix_gain_grad = own[:, 2 * value_part]

time: 845 us -> 601 us (0.71)
  waiting for transfers between devices: 528 us -> 286 us
  starting transfers between devices: 29.9 us -> 45.2 us
  matrix products: 62 us -> 53.2 us
    reduce_scatter x1, waiting for transfers between devices: 137 us -> 7.55 us  [body(): lax.psum_scatter(jnp.concatenate(parts, 2), 'dp', scatter_dimension=0, ax...]
    unnamed x7 -> x4, waiting for transfers between devices: 81.4 us -> 0.07 us
    all_gather x1 -> x0, waiting for transfers between devices: 38.9 us -> none  [body(): pack_first = lax.all_gather(pack_first, 'dp', axis=0, tiled=True)]
    ppermute x21 -> x33, waiting for transfers between devices: 134 us -> 171 us  [chip(): return lax.ppermute(t, 'dp', [(i, i ^ k) for i in range(ranks)])]
    all_gather x1, waiting for transfers between devices: 73.1 us -> 41.8 us  [body(): pack_feed = lax.all_gather(pack_feed, 'dp', axis=0, tiled=True)]
    ppermute x21 -> x33, starting transfers between devices: 27.4 us -> 42.1 us  [chip(): return lax.ppermute(t, 'dp', [(i, i ^ k) for i in range(ranks)])]
    add x0 -> x9, other arithmetic: none -> 13 us  [the longest x2 6.93 us: body(): part = grad[:, :width] + sibling(grad[:, width:].astype(BF16)).astype(F32)]
    convert_element_type x4 -> x3, other arithmetic: 12.8 us -> 1.26 us  [the longest x1 1 us: body(): parts = lax.psum_scatter(jnp.concatenate(parts, 2), 'dp', scatter_dimensi...]
  transfers between devices with their start and end apart: 39 -> 50, of which waited for: 21 -> 28; matrix products, arithmetic and copies ran while one was open for 17% -> 22% of each run, Pallas kernels for 2% -> 6%
where the time goes in v2:
time: 601 us; the launch traced here: 597 us
  waiting for transfers between devices  286 us (48%)
  Pallas kernels  87.3 us (15%)
  local copies, waits for them, and re-layouts  60.4 us (10%)
  matrix products  53.2 us (9%)
  other arithmetic  50 us (8%)
  starting transfers between devices  45.2 us (8%)
  between operations  14.8 us (2%)
    ppermute x33, waiting for transfers between devices, chip(): return lax.ppermute(t, 'dp', [(i, i ^ k) for i in range(ranks)])  171 us
    all_gather x1, waiting for transfers between devices, body(): table = lax.all_gather(table, 'dp', axis=0, axis_index_groups=lines)  63.3 us
    pallas_call x1, Pallas kernels, feed(): pl.pallas_call(feed_kernel, grid_spec=pltpu.PrefetchScalarGridSpec(num_sc...  54.3 us
    ppermute x33, starting transfers between devices, chip(): return lax.ppermute(t, 'dp', [(i, i ^ k) for i in range(ranks)])  42.1 us
    all_gather x1, waiting for transfers between devices, body(): pack_feed = lax.all_gather(pack_feed, 'dp', axis=0, tiled=True)  41.8 us
    pallas_call x1, Pallas kernels, mix_backward(): pl.pallas_call(mix_backward_kernel, grid_spec=pltpu.PrefetchScalarGridSpe...  18.6 us
    pallas_call x1, Pallas kernels, mix_forward(): pl.pallas_call(mix_forward_kernel, grid_spec=pltpu.PrefetchScalarGridSpec...  14.4 us
    dot_general x1, matrix products, body(): jnp.einsum('ti,tf->if', normed_feed, grad_up, preferred_element_type=F32)  13.4 us
  transfers between devices with their start and end apart: 50, of which 28 were waited for; matrix products, arithmetic and copies ran while one was open for 22% of the time, Pallas kernels for 6%

profile of v2, /device:TPU:0, one launch (start us, length us, event | category | flops | bytes accessed | tf_op | source)
XLA Modules:
  0.0 596.6 jit_solution(15995569317280248999)
XLA Ops:
  10.5 3.9 collective-permute-start.2
  15.1 5.1 collective-permute-done.2
  20.1 3.7 collective-permute-done.3
  26.0 63.3 %all-gather.3.cloned.1.call-done.ta = bf16[4,3,256,512]{3,2,1,0:T(8,128)(2,1)} async-done(((bf16[1,3,256,512]{3,2,1,0:T(8,128)(2,1)}), bf16[4,3,256,512]{3,2,1,0:T(8,128)(2,1)}) %all-gather.3.cloned.1.call-update) | async-done | bytes 3145744 | tf_op jit(solution)/shard_map/all_gather | solution.py:353
  90.7 4.8 collective-permute-done.6
  95.6 5.8 collective-permute-done.7
  103.2 8.9 %collective-permute-done.8 = bf16[2,2,48,896]{3,2,1,0:T(8,128)(2,1)S(1)} collective-permute-done((bf16[2,2,48,896]{3,2,1,0:T(8,128)(2,1)S(1)}, bf16[2,2,48,896]{3,2,1,0:T(8,128)(2,1)S(1)}, u32[]{:S(2)}, u32[]{:S(2)}) %collective-permute-start.8) | collective-permute-done | bytes 344096 | tf_op jit(solution)/shard_map/ppermute | solution.py:289
  119.2 19.3 %collective-permute-done.9 = bf16[2,2,2,48,896]{4,3,1,0,2:T(8,128)(2,1)} collective-permute-done((bf16[2,2,2,48,896]{4,3,1,0,2:T(8,128)(2,1)}, bf16[2,2,2,48,896]{4,3,1,0,2:T(8,128)(2,1)}, u32[]{:S(2)}, u32[]{:S(2)}) %collective-permute-start.9) | collective-permute-done | bytes 688160 | tf_op jit(solution)/shard_map/ppermute | solution.py:289
  151.4 41.8 %all-gather.5.cloned.1.call-done = bf16[768,3072]{1,0:T(8,128)(2,1)} async-done(((bf16[48,3072]{1,0:T(8,128)(2,1)}), bf16[768,3072]{1,0:T(8,128)(2,1)}) %all-gather.5.cloned.1.call-update) | async-done | bytes 4718608 | tf_op jit(solution)/shard_map/all_gather | solution.py:357
  193.2 3.9 constant_dynamic-slice_fusion.13
  213.3 30.2 %collective-permute-done.12.v2 = bf16[2,3,64,1024]{3,2,1,0:T(8,128)(2,1)} collective-permute-done((bf16[2,3,64,1024]{3,2,1,0:T(8,128)(2,1)}, bf16[2,3,64,1024]{3,2,1,0:T(8,128)(2,1)}, u32[]{:S(2)}, u32[]{:S(2)}) %collective-permute-start.12) | collective-permute-done | bytes 786464 | tf_op jit(solution)/shard_map/ppermute | solution.py:289
  243.4 14.4 %shard_map.169 = (bf16[2,3,64,1024]{3,2,1,0:T(8,128)(2,1)}, bf16[2,3,64,1024]{3,2,1,0:T(8,128)(2,1)}, bf16[2,3,64,1024]{3,2,1,0:T(8,128)(2,1)}, bf16[2,3,64,1024...) custom-call(s32[1]{0:T(128)} %bitcast.core, ...), custom_call_target="tpu_custom_call" | custom-call | flops 3271557120 | bytes 12582912 | tf_op jit(solution)/shard_map/pallas_call | solution.py:122
  262.1 4.9 fusion.9.grad
  267.0 12.7 %collective-permute-done.17 = bf16[2,3,64,1024]{3,2,1,0:T(8,128)(2,1)} collective-permute-done((bf16[2,3,64,1024]{3,2,1,0:T(8,128)(2,1)}, bf16[2,3,64,1024]{3,2,1,0:T(8,128)(2,1)}, u32[]{:S(2)}, u32[]{:S(2)}) %collective-permute-start.17) | collective-permute-done | bytes 786464 | tf_op jit(solution)/shard_map/ppermute | solution.py:289
  279.7 14.3 %collective-permute-done.18 = bf16[2,3,64,1024]{3,2,1,0:T(8,128)(2,1)} collective-permute-done((bf16[2,3,64,1024]{3,2,1,0:T(8,128)(2,1)}, bf16[2,3,64,1024]{3,2,1,0:T(8,128)(2,1)}, u32[]{:S(2)}, u32[]{:S(2)}) %collective-permute-start.18) | collective-permute-done | bytes 786464 | tf_op jit(solution)/shard_map/ppermute | solution.py:289
  298.4 7.0 %convert_add_fusion = f32[2,1024,768]{2,1,0:T(8,128)} fusion(bf16[2,768,1024]{2,1,0:T(8,128)(2,1)S(1)} %bitcast.238, bf16[768,384]{1,0:T(8,128)(2,1)S(1)} %copy-done.22, bf16[768,384]{1,0:T(8,128)(2,1)S(1)} %copy-done.21, pred[]{:T(512)S(6)} %eq.15, bf16[2,1024,384]{2,1,0:T(8,128)(2,1)S(1)} %get-tuple-element.84, ...), kind=kOutput, calls=%fused_computation.3 | convolution fusion | flops 2438529024 | bytes 13762561 | tf_op jit(solution)/shard_map/sct,oc->sto/dot_general | solution.py:390
  307.8 4.8 fusion.49
  312.7 54.3 %shard_map.170 = (bf16[2048,768]{1,0:T(8,128)(2,1)}, f32[2048,768]{1,0:T(8,128)}, bf16[2048,768]{1,0:T(8,128)(2,1)}, bf16[2048,3072]{1,0:T(8,128)(2,1)}, bf16[20...) custom-call(s32[2]{0:T(128)} %copy-done.29, f32[2048,768]{1,0:T(8,128)} %bitcast.267, ...), custom_call_target="tpu_custom_call" | custom-call | flops 38654705664 | bytes 59768832 | tf_op jit(solution)/shard_map/pallas_call | solution.py:236
  367.0 5.4 convolution_convert_fusion
  377.2 13.4 %fusion.53 = f32[768,3072]{1,0:T(8,128)S(1)} fusion(bf16[2048,768]{1,0:T(8,128)(2,1)S(1)} %copy-done.38, bf16[2048,3072]{1,0:T(8,128)(2,1)} %get-tuple-element.49), kind=kOutput, calls=%fused_computation.182 | convolution fusion | flops 9663676416 | bytes 25165824 | tf_op jit(solution)/shard_map/ti,tf->if/dot_general | solution.py:419
  394.8 4.0 convolution_bitcast_fusion
  398.8 11.2 %collective-permute-done.24.g2 = bf16[2,3,64,1024]{3,2,1,0:T(8,128)(2,1)S(1)} collective-permute-done((bf16[2,3,64,1024]{3,2,1,0:T(8,128)(2,1)S(1)}, bf16[2,3,64,1024]{3,2,1,0:T(8,128)(2,1)S(1)}, u32[]{:S(2)}, u32[]{:S(2)}) %collective-permute-start.24) | collective-permute-done | bytes 786464 | tf_op jit(solution)/shard_map/ppermute | solution.py:289
  411.2 18.6 %shard_map.171 = (bf16[4,3,256,512]{3,2,1,0:T(8,128)(2,1)}, bf16[4,3,256,512]{3,2,1,0:T(8,128)(2,1)}, bf16[2,3,64,1024]{3,2,1,0:T(8,128)(2,1)}, bf16[2,3,64,1024...) custom-call(s32[1]{0:T(128)} %bitcast.core, ...), custom_call_target="tpu_custom_call" | custom-call | flops 6543114240 | bytes 12582912 | tf_op jit(solution)/shard_map/pallas_call | solution.py:152
  433.3 12.9 %fusion.54 = f32[768,3072]{1,0:T(8,128)S(1)} fusion(bf16[2048,768]{1,0:T(8,128)(2,1)S(1)} %copy-done.10, bf16[2048,3072]{1,0:T(8,128)(2,1)} %get-tuple-element.50), kind=kOutput, calls=%fused_computation.183 | convolution fusion | flops 9663676416 | bytes 25165824 | tf_op jit(solution)/shard_map/ti,tf->if/dot_general | solution.py:420
  458.2 7.3 %collective-permute-done.27 = bf16[2,3,64,1024]{3,2,1,0:T(8,128)(2,1)} collective-permute-done((bf16[2,3,64,1024]{3,2,1,0:T(8,128)(2,1)}, bf16[2,3,64,1024]{3,2,1,0:T(8,128)(2,1)}, u32[]{:S(2)}, u32[]{:S(2)}) %collective-permute-start.27) | collective-permute-done | bytes 786464 | tf_op jit(solution)/shard_map/ppermute | solution.py:289
  469.3 4.5 fusion.8
  490.8 4.4 slice_add_fusion.1
  510.7 15.0 %collective-permute-done.41 = bf16[4,2,48,1536]{3,2,0,1:T(8,128)(2,1)} collective-permute-done((bf16[4,2,48,1536]{3,2,0,1:T(8,128)(2,1)}, bf16[4,2,48,1536]{3,2,0,1:T(8,128)(2,1)}, u32[]{:S(2)}, u32[]{:S(2)}) %collective-permute-start.41) | collective-permute-done | bytes 1179680 | tf_op jit(solution)/shard_map/ppermute | solution.py:289
  535.5 4.9 collective-permute-done.31
  545.1 7.3 %collective-permute-done.45 = bf16[4,48,1536]{2,1,0:T(8,128)(2,1)S(1)} collective-permute-done((bf16[4,48,1536]{2,1,0:T(8,128)(2,1)S(1)}, bf16[4,48,1536]{2,1,0:T(8,128)(2,1)S(1)}, u32[]{:S(2)}, u32[]{:S(2)}) %collective-permute-start.45) | collective-permute-done | bytes 589856 | tf_op jit(solution)/shard_map/ppermute | solution.py:289
  565.7 5.0 collective-permute-done.34
  576.9 7.6 %reduce-scatter.5.cloned.1.call-done = bf16[1,48,3072]{2,1,0:T(8,128)(2,1)} async-done(((bf16[4,48,3072]{2,1,0:T(8,128)(2,1)}), bf16[1,48,3072]{2,1,0:T(8,128)(2,1)}) %reduce-scatter.5.cloned.1.call-update) | async-done | bytes 294928 | tf_op jit(solution)/shard_map/reduce_scatter | solution.py:428
  (272 shorter events, 157.2 us)
Async XLA Ops:
  7.2 82.1 %all-gather.3.cloned.1.call-start = ((), (), s32[]{:S(2)}) async-start(), calls=%async_computation.2 | async-start | bytes 3932160 | tf_op jit(solution)/shard_map/all_gather | solution.py:353
  25.2 168.0 %all-gather.5.cloned.1.call-start = ((), (), s32[]{:S(2)}) async-start(), calls=%async_computation.3 | async-start | bytes 5013504 | tf_op jit(solution)/shard_map/all_gather | solution.py:357
  89.3 482.8 %reduce-scatter.3.cloned.1.call-start = ((), (), s32[]{:S(2)}) async-start(), calls=%async_computation.4 | async-start | bytes 3932160 | tf_op jit(solution)/shard_map/reduce_scatter | solution.py:410
  113.1 25.4 %collective-permute-start.9 = (bf16[2,2,2,48,896]{4,3,1,0,2:T(8,128)(2,1)}, bf16[2,2,2,48,896]{4,3,1,0,2:T(8,128)(2,1)}, u32[]{:S(2)}, u32[]{:S(2)}) collective-permute-start(bf16[2,2,2,48,896]{4,3,1,0,2:T(8,128)(2,1)} %maximum_select_fusion.9), channel_id=1, source_target_pairs={{0,2},{2,0},{4,6},{6,4},{8,10},{10,8},{12,14},{14,12},{16,18},{18,... | collective-permute-start | bytes 2064392 | tf_op jit(solution)/shard_map/ppermute | solution.py:289
  118.0 23.4 %collective-permute-start = (bf16[2,1024,384]{2,1,0:T(8,128)(2,1)}, bf16[2,1024,384]{2,1,0:T(8,128)(2,1)S(1)}, u32[]{:S(2)}, u32[]{:S(2)}) collective-permute-start(bf16[2,1024,384]{2,1,0:T(8,128)(2,1)} %get-tuple-element.83), channel_id=1, source_target_pairs={{0,1},{1,0},{2,3},{3,2},{4,5},{5,4},{6,7},{7,6},{8,9},{9,8},{10,11... | collective-permute-start | bytes 4718600 | tf_op jit(solution)/shard_map/ppermute | solution.py:286
  142.8 100.7 %collective-permute-start.5 = (bf16[4,3,256,512]{3,2,1,0:T(8,128)(2,1)}, bf16[4,3,256,512]{3,2,1,0:T(8,128)(2,1)}, u32[]{:S(2)}, u32[]{:S(2)}) collective-permute-start(bf16[4,3,256,512]{3,2,1,0:T(8,128)(2,1)} %all-gather.3.cloned.1.call-done.ta), channel_id=1, source_target_pairs={{0,1},{1,0},{2,3},{3,2},{4,5},{5,4},{6,7},{7,6},{8,9},{9,8},{10,11... | collective-permute-start | bytes 9437192 | tf_op jit(solution)/shard_map/ppermute | solution.py:286
  149.7 62.3 %collective-permute-start.11 = (bf16[2,3,64,1024]{3,2,1,0:T(8,128)(2,1)}, bf16[2,3,64,1024]{3,2,1,0:T(8,128)(2,1)}, u32[]{:S(2)}, u32[]{:S(2)}) collective-permute-start(bf16[2,3,64,1024]{3,2,1,0:T(8,128)(2,1)} %get-tuple-element.81), channel_id=1, source_target_pairs={{0,2},{2,0},{4,6},{6,4},{8,10},{10,8},{12,14},{14,12},{16,18},{18,... | collective-permute-start | bytes 2359304 | tf_op jit(solution)/shard_map/ppermute | solution.py:289
  193.2 114.6 %collective-permute-start.21 = (bf16[768,3072]{1,0:T(8,128)(2,1)}, bf16[768,3072]{1,0:T(8,128)(2,1)}, u32[]{:S(2)}, u32[]{:S(2)}) collective-permute-start(bf16[768,3072]{1,0:T(8,128)(2,1)} %all-gather.5.cloned.1.call-done), channel_id=1, source_target_pairs={{0,1},{1,0},{2,3},{3,2},{4,5},{5,4},{6,7},{7,6},{8,9},{9,8},{10,11... | collective-permute-start | bytes 14155784 | tf_op jit(solution)/shard_map/ppermute | solution.py:286
  197.1 65.0 %collective-permute-start.20 = (bf16[2,1024,384]{2,1,0:T(8,128)(2,1)}, bf16[2,1024,384]{2,1,0:T(8,128)(2,1)}, u32[]{:S(2)}, u32[]{:S(2)}) collective-permute-start(bf16[2,1024,384]{2,1,0:T(8,128)(2,1)} %get-tuple-element.74), channel_id=1, source_target_pairs={{0,1},{1,0},{2,3},{3,2},{4,5},{5,4},{6,7},{7,6},{8,9},{9,8},{10,11... | collective-permute-start | bytes 4718600 | tf_op jit(solution)/shard_map/ppermute | solution.py:286
  210.0 33.5 %collective-permute-start.12 = (bf16[2,3,64,1024]{3,2,1,0:T(8,128)(2,1)}, bf16[2,3,64,1024]{3,2,1,0:T(8,128)(2,1)}, u32[]{:S(2)}, u32[]{:S(2)}) collective-permute-start(bf16[2,3,64,1024]{3,2,1,0:T(8,128)(2,1)} %get-tuple-element.80), channel_id=1, source_target_pairs={{0,4},{2,6},{4,0},{6,2},{8,12},{10,14},{12,8},{14,10},{16,20},{18,... | collective-permute-start | bytes 2359304 | tf_op jit(solution)/shard_map/ppermute | solution.py:289
  212.0 31.4 %collective-permute-start.13 = (bf16[2,3,64,1024]{3,2,1,0:T(8,128)(2,1)}, bf16[2,3,64,1024]{3,2,1,0:T(8,128)(2,1)}, u32[]{:S(2)}, u32[]{:S(2)}) collective-permute-start(bf16[2,3,64,1024]{3,2,1,0:T(8,128)(2,1)} %get-tuple-element.79), channel_id=1, source_target_pairs={{0,6},{2,4},{4,2},{6,0},{8,14},{10,12},{12,10},{14,8},{16,22},{18,... | collective-permute-start | bytes 2359304 | tf_op jit(solution)/shard_map/ppermute | solution.py:289
  257.9 21.8 %collective-permute-start.17 = (bf16[2,3,64,1024]{3,2,1,0:T(8,128)(2,1)}, bf16[2,3,64,1024]{3,2,1,0:T(8,128)(2,1)}, u32[]{:S(2)}, u32[]{:S(2)}) collective-permute-start(bf16[2,3,64,1024]{3,2,1,0:T(8,128)(2,1)} %get-tuple-element.31.x3), channel_id=1, source_target_pairs={{0,6},{2,4},{4,2},{6,0},{8,14},{10,12},{12,10},{14,8},{16,22},{18,... | collective-permute-start | bytes 2359304 | tf_op jit(solution)/shard_map/ppermute | solution.py:289
  260.1 33.9 %collective-permute-start.18 = (bf16[2,3,64,1024]{3,2,1,0:T(8,128)(2,1)}, bf16[2,3,64,1024]{3,2,1,0:T(8,128)(2,1)}, u32[]{:S(2)}, u32[]{:S(2)}) collective-permute-start(bf16[2,3,64,1024]{3,2,1,0:T(8,128)(2,1)} %get-tuple-element.32.x2), channel_id=1, source_target_pairs={{0,4},{2,6},{4,0},{6,2},{8,12},{10,14},{12,8},{14,10},{16,20},{18,... | collective-permute-start | bytes 2359304 | tf_op jit(solution)/shard_map/ppermute | solution.py:289
  260.4 34.5 %collective-permute-start.19 = (bf16[2,3,64,1024]{3,2,1,0:T(8,128)(2,1)}, bf16[2,3,64,1024]{3,2,1,0:T(8,128)(2,1)}, u32[]{:S(2)}, u32[]{:S(2)}) collective-permute-start(bf16[2,3,64,1024]{3,2,1,0:T(8,128)(2,1)} %get-tuple-element.33.x1), channel_id=1, source_target_pairs={{0,2},{2,0},{4,6},{6,4},{8,10},{10,8},{12,14},{14,12},{16,18},{18,... | collective-permute-start | bytes 2359304 | tf_op jit(solution)/shard_map/ppermute | solution.py:289
  373.7 25.1 %collective-permute-start.23 = (bf16[2,3,64,1024]{3,2,1,0:T(8,128)(2,1)S(1)}, bf16[2,3,64,1024]{3,2,1,0:T(8,128)(2,1)S(1)}, u32[]{:S(2)}, u32[]{:S(2)}) collective-permute-start(bf16[2,3,64,1024]{3,2,1,0:T(8,128)(2,1)S(1)} %get-tuple-element.69), channel_id=1, source_target_pairs={{0,2},{2,0},{4,6},{6,4},{8,10},{10,8},{12,14},{14,12},{16,18},{18,... | collective-permute-start | bytes 2359304 | tf_op jit(solution)/shard_map/ppermute | solution.py:289
  374.6 35.3 %collective-permute-start.24 = (bf16[2,3,64,1024]{3,2,1,0:T(8,128)(2,1)S(1)}, bf16[2,3,64,1024]{3,2,1,0:T(8,128)(2,1)S(1)}, u32[]{:S(2)}, u32[]{:S(2)}) collective-permute-start(bf16[2,3,64,1024]{3,2,1,0:T(8,128)(2,1)S(1)} %get-tuple-element.68), channel_id=1, source_target_pairs={{0,4},{2,6},{4,0},{6,2},{8,12},{10,14},{12,8},{14,10},{16,20},{18,... | collective-permute-start | bytes 2359304 | tf_op jit(solution)/shard_map/ppermute | solution.py:289
  375.6 34.3 %collective-permute-start.25 = (bf16[2,3,64,1024]{3,2,1,0:T(8,128)(2,1)S(1)}, bf16[2,3,64,1024]{3,2,1,0:T(8,128)(2,1)S(1)}, u32[]{:S(2)}, u32[]{:S(2)}) collective-permute-start(bf16[2,3,64,1024]{3,2,1,0:T(8,128)(2,1)S(1)} %get-tuple-element.67), channel_id=1, source_target_pairs={{0,6},{2,4},{4,2},{6,0},{8,14},{10,12},{12,10},{14,8},{16,22},{18,... | collective-permute-start | bytes 2359304 | tf_op jit(solution)/shard_map/ppermute | solution.py:289
  392.3 98.5 %collective-permute-start.40 = (bf16[768,1536]{1,0:T(8,128)(2,1)}, bf16[768,1536]{1,0:T(8,128)(2,1)}, u32[]{:S(2)}, u32[]{:S(2)}) collective-permute-start(bf16[768,1536]{1,0:T(8,128)(2,1)} %slice.113), channel_id=1, source_target_pairs={{0,1},{1,0},{2,3},{3,2},{4,5},{5,4},{6,7},{7,6},{8,9},{9,8},{10,11... | collective-permute-start | bytes 7077896 | tf_op jit(solution)/shard_map/ppermute | solution.py:286
  429.7 27.9 %collective-permute-start.26 = (bf16[2,3,64,1024]{3,2,1,0:T(8,128)(2,1)}, bf16[2,3,64,1024]{3,2,1,0:T(8,128)(2,1)}, u32[]{:S(2)}, u32[]{:S(2)}) collective-permute-start(bf16[2,3,64,1024]{3,2,1,0:T(8,128)(2,1)} %get-tuple-element.41), channel_id=1, source_target_pairs={{0,6},{2,4},{4,2},{6,0},{8,14},{10,12},{12,10},{14,8},{16,22},{18,... | collective-permute-start | bytes 2359304 | tf_op jit(solution)/shard_map/ppermute | solution.py:289
  431.4 34.1 %collective-permute-start.27 = (bf16[2,3,64,1024]{3,2,1,0:T(8,128)(2,1)}, bf16[2,3,64,1024]{3,2,1,0:T(8,128)(2,1)}, u32[]{:S(2)}, u32[]{:S(2)}) collective-permute-start(bf16[2,3,64,1024]{3,2,1,0:T(8,128)(2,1)} %get-tuple-element.42), channel_id=1, source_target_pairs={{0,4},{2,6},{4,0},{6,2},{8,12},{10,14},{12,8},{14,10},{16,20},{18,... | collective-permute-start | bytes 2359304 | tf_op jit(solution)/shard_map/ppermute | solution.py:289
  432.0 33.5 %collective-permute-start.28 = (bf16[2,3,64,1024]{3,2,1,0:T(8,128)(2,1)}, bf16[2,3,64,1024]{3,2,1,0:T(8,128)(2,1)}, u32[]{:S(2)}, u32[]{:S(2)}) collective-permute-start(bf16[2,3,64,1024]{3,2,1,0:T(8,128)(2,1)} %get-tuple-element.43), channel_id=1, source_target_pairs={{0,2},{2,0},{4,6},{6,4},{8,10},{10,8},{12,14},{14,12},{16,18},{18,... | collective-permute-start | bytes 2359304 | tf_op jit(solution)/shard_map/ppermute | solution.py:289
  451.6 45.8 %collective-permute-start.43 = (bf16[768,1536]{1,0:T(8,128)(2,1)}, bf16[768,1536]{1,0:T(8,128)(2,1)}, u32[]{:S(2)}, u32[]{:S(2)}) collective-permute-start(bf16[768,1536]{1,0:T(8,128)(2,1)} %slice.112), channel_id=1, source_target_pairs={{0,1},{1,0},{2,3},{3,2},{4,5},{5,4},{6,7},{7,6},{8,9},{9,8},{10,11... | collective-permute-start | bytes 7077896 | tf_op jit(solution)/shard_map/ppermute | solution.py:286
  457.6 98.0 %collective-permute-start.22 = (bf16[2,1024,384]{2,1,0:T(8,128)(2,1)}, bf16[2,1024,384]{2,1,0:T(8,128)(2,1)}, u32[]{:S(2)}, u32[]{:S(2)}) collective-permute-start(bf16[2,1024,384]{2,1,0:T(8,128)(2,1)} %get-tuple-element.72), channel_id=1, source_target_pairs={{0,1},{1,0},{2,3},{3,2},{4,5},{5,4},{6,7},{7,6},{8,9},{9,8},{10,11... | collective-permute-start | bytes 4718600 | tf_op jit(solution)/shard_map/ppermute | solution.py:286
  465.4 16.8 %collective-permute-start.35 = (bf16[4,3,256,512]{3,2,1,0:T(8,128)(2,1)S(1)}, bf16[4,3,256,512]{3,2,1,0:T(8,128)(2,1)S(1)}, u32[]{:S(2)}, u32[]{:S(2)}) collective-permute-start(bf16[4,3,256,512]{3,2,1,0:T(8,128)(2,1)S(1)} %copy-done.30), channel_id=1, source_target_pairs={{0,1},{1,0},{2,3},{3,2},{4,5},{5,4},{6,7},{7,6},{8,9},{9,8},{10,11... | collective-permute-start | bytes 9437192 | tf_op jit(solution)/shard_map/ppermute | solution.py:286
  478.2 26.1 %collective-permute-start.30 = (bf16[768,896]{0,1:T(8,128)(2,1)}, bf16[768,896]{0,1:T(8,128)(2,1)}, u32[]{:S(2)}, u32[]{:S(2)}) collective-permute-start(bf16[768,896]{0,1:T(8,128)(2,1)} %pad_maximum_fusion.2), channel_id=1, source_target_pairs={{0,1},{1,0},{2,3},{3,2},{4,5},{5,4},{6,7},{7,6},{8,9},{9,8},{10,11... | collective-permute-start | bytes 4128776 | tf_op jit(solution)/shard_map/ppermute | solution.py:286
  485.0 99.4 %reduce-scatter.5.cloned.1.call-start = ((), (), s32[]{:S(2)}) async-start(), calls=%async_computation.5 | async-start | bytes 1474560 | tf_op jit(solution)/shard_map/reduce_scatter | solution.py:428
  488.9 73.3 %collective-permute-start.29 = (bf16[2,1024,384]{2,1,0:T(8,128)(2,1)}, bf16[2,1024,384]{2,1,0:T(8,128)(2,1)}, u32[]{:S(2)}, u32[]{:S(2)}) collective-permute-start(bf16[2,1024,384]{2,1,0:T(8,128)(2,1)} %get-tuple-element.62), channel_id=1, source_target_pairs={{0,1},{1,0},{2,3},{3,2},{4,5},{5,4},{6,7},{7,6},{8,9},{9,8},{10,11... | collective-permute-start | bytes 4718600 | tf_op jit(solution)/shard_map/ppermute | solution.py:286
  496.6 29.1 %collective-permute-start.41 = (bf16[4,2,48,1536]{3,2,0,1:T(8,128)(2,1)}, bf16[4,2,48,1536]{3,2,0,1:T(8,128)(2,1)}, u32[]{:S(2)}, u32[]{:S(2)}) collective-permute-start(bf16[4,2,48,1536]{3,2,0,1:T(8,128)(2,1)} %fusion.19), channel_id=1, source_target_pairs={{0,2},{2,0},{4,6},{6,4},{8,10},{10,8},{12,14},{14,12},{16,18},{18,... | collective-permute-start | bytes 3538952 | tf_op jit(solution)/shard_map/ppermute | solution.py:289
  503.3 29.1 %collective-permute-start.44 = (bf16[4,2,48,1536]{3,2,0,1:T(8,128)(2,1)}, bf16[4,2,48,1536]{3,2,0,1:T(8,128)(2,1)}, u32[]{:S(2)}, u32[]{:S(2)}) collective-permute-start(bf16[4,2,48,1536]{3,2,0,1:T(8,128)(2,1)} %fusion.20), channel_id=1, source_target_pairs={{0,4},{2,6},{4,0},{6,2},{8,12},{10,14},{12,8},{14,10},{16,20},{18,... | collective-permute-start | bytes 3538952 | tf_op jit(solution)/shard_map/ppermute | solution.py:289
  509.8 30.5 %collective-permute-start.31 = (bf16[2,2,2,48,896]{4,3,2,1,0:T(8,128)(2,1)S(1)}, bf16[2,2,2,48,896]{4,3,2,1,0:T(8,128)(2,1)S(1)}, u32[]{:S(2)}, u32[]{:S(2)}) collective-permute-start(bf16[2,2,2,48,896]{4,3,2,1,0:T(8,128)(2,1)S(1)} %fusion.31), channel_id=1, source_target_pairs={{0,2},{2,0},{4,6},{6,4},{8,10},{10,8},{12,14},{14,12},{16,18},{18,... | collective-permute-start | bytes 2064392 | tf_op jit(solution)/shard_map/ppermute | solution.py:289
  528.2 16.8 %collective-permute-start.42 = (bf16[4,48,1536]{2,1,0:T(8,128)(2,1)S(1)}, bf16[4,48,1536]{2,1,0:T(8,128)(2,1)S(1)}, u32[]{:S(2)}, u32[]{:S(2)}) collective-permute-start(bf16[4,48,1536]{2,1,0:T(8,128)(2,1)S(1)} %fusion.32), channel_id=1, source_target_pairs={{0,4},{2,6},{4,0},{6,2},{8,12},{10,14},{12,8},{14,10},{16,20},{18,... | collective-permute-start | bytes 1769480 | tf_op jit(solution)/shard_map/ppermute | solution.py:289
  534.2 18.2 %collective-permute-start.45 = (bf16[4,48,1536]{2,1,0:T(8,128)(2,1)S(1)}, bf16[4,48,1536]{2,1,0:T(8,128)(2,1)S(1)}, u32[]{:S(2)}, u32[]{:S(2)}) collective-permute-start(bf16[4,48,1536]{2,1,0:T(8,128)(2,1)S(1)} %fusion.33), channel_id=1, source_target_pairs={{0,2},{2,0},{4,6},{6,4},{8,10},{10,8},{12,14},{14,12},{16,18},{18,... | collective-permute-start | bytes 1769480 | tf_op jit(solution)/shard_map/ppermute | solution.py:289
  (64 other events, 816.0 us)
Sparse Core Ops, SparseCore 0:
  25.3 63.9 all-gather.2
  92.7 100.4 all-gather.4
  485.2 60.7 reduce-scatter.2
  553.8 30.5 reduce-scatter.4
